TPU v7x, 512 devices: a whole 4x8x8 slice. The times are simulated.
512 devices in a mesh: dp: 16 (over z, core), dom: 32 (over x, y).
Axes of the slice: x: 4, y: 8, z: 8, core: 2. Of those that a mesh axis runs over, the one named last changes fastest.
Arguments:
- nodes: bfloat16 [16, 65536, 128], P('dp', 'dom'), may hold values from -6 to 6
- cotangent: bfloat16 [16, 65536, 128], P('dp', 'dom'), may hold values from -6 to 6
- weights: bfloat16 [3, 4, 128, 128], replicated, may hold values from -0.5 to 0.5
- fine_tiles: bfloat16 [512, 3, 128, 128], P('dom'), may hold values from -0.3125 to 0.3125
- fine_cols: int32 [512, 3], P('dom'), may hold values from 0 to 17, as said below
- fine_export: int32 [32, 2, 128], P('dom'), may hold values from 0 to 2047
- pool_tiles: bfloat16 [128, 2, 128, 128], P('dom'), may hold values from -0.375 to 0.375
- pool_cols: int32 [128, 2], P('dom'), may hold values from 0 to 15
- mid_tiles: bfloat16 [128, 3, 128, 128], P('dom'), may hold values from -0.3125 to 0.3125
- mid_cols: int32 [128, 3], P('dom'), may hold values from 0 to 5, as said below
- mid_export: int32 [32, 2, 128], P('dom'), may hold values from 0 to 511
- top_pool_tiles: bfloat16 [32, 2, 128, 128], P('dom'), may hold values from -0.375 to 0.375
- top_pool_cols: int32 [32, 2], P('dom'), may hold values from 0 to 3
- top_tiles: bfloat16 [32, 3, 128, 128], P('dom'), may hold values from -1 to 1
- top_cols: int32 [32, 3], P('dom'), may hold values from 0 to 31, as said below
Outputs:
- node_grad: bfloat16 [16, 65536, 128], P('dp', 'dom')
- weight_grad: float32 [3, 4, 128, 128], replicated
Inputs may be any that keep to these rules, and one draw needn't show every extreme that they name: `fine_cols`: tile 0 of every fine row block is the block itself; tile 2 of a partition's first row block is block 16, of its last row block block 17. `mid_cols`: tile 0 of every middle row block is the block itself; tile 2 of a partition's first row block is block 4, of its last row block block 5. `top_cols`: tile 0 of every coarsest row block r is r itself, tile 1 is block (r + 16) modulo 32.
All inputs are finite; a program needn't handle non-finite values.
Results may differ from a plain program's by a relative error of at most 0.015.
Values may be sent and summed in bfloat16 or wider, within the bound.
A program may use at most 64 MiB of HBM per device.

v0:
```python
import jax
import jax.numpy as jnp
from jax import lax
from jax.sharding import PartitionSpec as P


def extended_2(cells, sides, width):
    for axis, dim in sides:
        count = lax.axis_size(axis)
        ends = count - 1
        head = lax.slice_in_dim(cells, 0, width, axis=dim)
        tail = lax.slice_in_dim(cells, cells.shape[dim] - width, cells.shape[dim], axis=dim)
        cells = jnp.concatenate(
            [
                lax.ppermute(tail, axis, [(i, (i + 1) % count) for i in range(ends)]),
                cells,
                lax.ppermute(head, axis, [((i + 1) % count, i) for i in range(ends)]),
            ],
            axis=dim,
        )
    return cells


def silu_slope(pre_values):
    logistic = jax.nn.sigmoid(pre_values)
    return logistic * (1.0 + pre_values * (1.0 - logistic))


def mixed(left, right):
    return jnp.einsum("srw,wv->srv", left, right, preferred_element_type=jnp.float32)


def mixed_back(left, right):
    return jnp.einsum("srv,wv->srw", left, right, preferred_element_type=jnp.float32)


def outer_sum(left, right):
    return jnp.einsum("srw,srv->wv", left, right, preferred_element_type=jnp.float32)


def node_forward(inputs, message, matrices):
    first_pre = mixed(inputs, matrices[0]) + mixed(message, matrices[1])
    first_act = jax.nn.silu(first_pre).astype(jnp.bfloat16)
    second_pre = mixed(first_act, matrices[2])
    second_act = jax.nn.silu(second_pre).astype(jnp.bfloat16)
    output = (inputs.astype(jnp.float32) + mixed(second_act, matrices[3])).astype(jnp.bfloat16)
    return (output, (first_pre, first_act, second_pre, second_act))


def node_backward(grad_out, inputs, message, saved, matrices):
    first_pre, first_act, second_pre, second_act = saved
    grad_low = grad_out.astype(jnp.bfloat16)
    grad_last = outer_sum(second_act, grad_low)
    grad_second = (mixed_back(grad_low, matrices[3]) * silu_slope(second_pre)).astype(jnp.bfloat16)
    grad_hidden = outer_sum(first_act, grad_second)
    grad_first = (mixed_back(grad_second, matrices[2]) * silu_slope(first_pre)).astype(jnp.bfloat16)
    grad_node = outer_sum(inputs, grad_first)
    grad_mess = outer_sum(message, grad_first)
    grad_inputs = grad_out + mixed_back(grad_first, matrices[0])
    grad_message = mixed_back(grad_first, matrices[1])
    return (grad_inputs, grad_message, jnp.stack([grad_node, grad_mess, grad_hidden, grad_last]))


def blockify(values, tile_rows):
    return values.reshape(values.shape[0], -1, tile_rows, values.shape[-1])


def tile_apply(adjacency, columns, blocks):
    picked = blocks[:, columns]
    return jnp.einsum("bkij,sbkjw->sbiw", adjacency, picked, preferred_element_type=jnp.float32)


def tile_spread(adjacency, columns, gradient, number):
    pieces = jnp.einsum("bkij,sbiw->bksjw", adjacency, gradient, preferred_element_type=jnp.float32)
    blocks, per_row, snaps, tile_rows, width = pieces.shape
    flat = pieces.reshape(blocks * per_row, snaps, tile_rows, width)
    summed = jax.ops.segment_sum(flat, columns.reshape(-1), num_segments=number)
    return jnp.transpose(summed, (1, 0, 2, 3))


def with_halo(values, export, level_fine):
    sent = jnp.stack([values[:, export[0, 0]], values[:, export[0, 1]]], 0)
    if level_fine:
        extended = extended_2(sent, (("dom", 0),), 1)
    else:
        extended = extended_2(sent, (("dom", 0),), 1)
    blocks = blockify(values, export.shape[-1])
    return jnp.concatenate([blocks, extended[0][:, None], extended[3][:, None]], 1)


def halo_back(gradient, export, local_blocks, level_fine):
    stacked = jnp.stack([gradient[:, local_blocks], gradient[:, local_blocks + 1]], 0)
    if level_fine:
        extended = extended_2(stacked, (("dom", 0),), 1)
    else:
        extended = extended_2(stacked, (("dom", 0),), 1)
    snaps = gradient.shape[0]
    own = gradient[:, :local_blocks].reshape(snaps, -1, gradient.shape[-1])
    return own.at[:, export[0, 0]].add(extended[0]).at[:, export[0, 1]].add(extended[3])


def on_device(
    nodes,
    cotangent,
    weights,
    fine_tiles,
    fine_cols,
    fine_export,
    pool_tiles,
    pool_cols,
    mid_tiles,
    mid_cols,
    mid_export,
    top_pool_tiles,
    top_pool_cols,
    top_tiles,
    top_cols,
):
    snaps, fine_rows, width = nodes.shape
    tile_rows = fine_tiles.shape[-1]
    fine_blocks = fine_tiles.shape[0]
    mid_blocks = pool_tiles.shape[0]
    mid_rows = mid_blocks * tile_rows
    top_rows = top_pool_tiles.shape[0] * tile_rows
    fine_msg = (
        tile_apply(fine_tiles, fine_cols, with_halo(nodes, fine_export, True))
        .reshape(snaps, fine_rows, width)
        .astype(jnp.bfloat16)
    )
    fine_out, fine_saved = node_forward(nodes, fine_msg, weights[0])
    mid_in = (
        tile_apply(pool_tiles, pool_cols, blockify(fine_out, tile_rows))
        .reshape(snaps, mid_rows, width)
        .astype(jnp.bfloat16)
    )
    mid_msg = (
        tile_apply(mid_tiles, mid_cols, with_halo(mid_in, mid_export, False))
        .reshape(snaps, mid_rows, width)
        .astype(jnp.bfloat16)
    )
    mid_out, mid_saved = node_forward(mid_in, mid_msg, weights[1])
    top_in = (
        tile_apply(top_pool_tiles, top_pool_cols, blockify(mid_out, tile_rows))
        .reshape(snaps, top_rows, width)
        .astype(jnp.bfloat16)
    )
    every_top = lax.all_gather(top_in, "dom", axis=1, tiled=True)
    total_top = every_top.shape[1] // tile_rows
    top_msg = (
        tile_apply(top_tiles, top_cols, blockify(every_top, tile_rows))
        .reshape(snaps, top_rows, width)
        .astype(jnp.bfloat16)
    )
    top_out, top_saved = node_forward(top_in, top_msg, weights[2])
    grad_mid = tile_apply(pool_tiles, pool_cols, blockify(cotangent, tile_rows)).reshape(
        snaps, mid_rows, width
    )
    grad_top = tile_apply(
        top_pool_tiles, top_pool_cols, blockify(grad_mid.astype(jnp.bfloat16), tile_rows)
    ).reshape(snaps, top_rows, width)
    grad_top_in, grad_top_msg, top_terms = node_backward(
        grad_top, top_in, top_msg, top_saved, weights[2]
    )
    spread_top = tile_spread(
        top_tiles, top_cols, blockify(grad_top_msg.astype(jnp.bfloat16), tile_rows), total_top
    )
    returned = lax.psum_scatter(
        spread_top.reshape(snaps, -1, width), "dom", scatter_dimension=1, tiled=True
    )
    grad_top_in = grad_top_in + returned
    grad_mid = grad_mid + tile_spread(
        top_pool_tiles,
        top_pool_cols,
        blockify(grad_top_in.astype(jnp.bfloat16), tile_rows),
        mid_blocks,
    ).reshape(snaps, mid_rows, width)
    grad_mid_in, grad_mid_msg, mid_terms = node_backward(
        grad_mid, mid_in, mid_msg, mid_saved, weights[1]
    )
    mid_spread = tile_spread(
        mid_tiles, mid_cols, blockify(grad_mid_msg.astype(jnp.bfloat16), tile_rows), mid_blocks + 2
    )
    grad_mid_in = grad_mid_in + halo_back(mid_spread, mid_export, mid_blocks, False)
    grad_fine = cotangent.astype(jnp.float32) + tile_spread(
        pool_tiles, pool_cols, blockify(grad_mid_in.astype(jnp.bfloat16), tile_rows), fine_blocks
    ).reshape(snaps, fine_rows, width)
    grad_nodes, grad_fine_msg, fine_terms = node_backward(
        grad_fine, nodes, fine_msg, fine_saved, weights[0]
    )
    fine_spread = tile_spread(
        fine_tiles,
        fine_cols,
        blockify(grad_fine_msg.astype(jnp.bfloat16), tile_rows),
        fine_blocks + 2,
    )
    grad_nodes = grad_nodes + halo_back(fine_spread, fine_export, fine_blocks, True)
    weight_grad = jnp.stack([fine_terms, mid_terms, top_terms])
    weight_grad = lax.psum(weight_grad, ("dp", "dom"))
    return (grad_nodes.astype(jnp.bfloat16), weight_grad)


def solution(mesh):
    return jax.shard_map(
        on_device,
        mesh=mesh,
        in_specs=(
            P("dp", "dom", None),
            P("dp", "dom", None),
            P(),
            P("dom", None, None, None),
            P("dom", None),
            P("dom", None, None),
            P("dom", None, None, None),
            P("dom", None),
            P("dom", None, None, None),
            P("dom", None),
            P("dom", None, None),
            P("dom", None, None, None),
            P("dom", None),
            P("dom", None, None, None),
            P("dom", None),
        ),
        out_specs=(P("dp", "dom", None), P()),
        check_vma=False,
    )
```

profile of v0, /device:TPU:1, one launch (start us, length us, event | category | flops | bytes accessed | tf_op | source)
XLA Modules:
  0.0 702.8 jit_solution(16836185488134311169)
XLA Ops:
  8.1 1.8 gather_fusion.2
  9.9 4.0 collective-permute-start
  13.9 1.8 gather_fusion.3
  15.7 1.3 collective-permute-start.1
  17.9 2.3 fusion.76
  20.7 2.0 gather_fusion.4
  22.7 2.1 fusion.7
  24.8 2.2 multiply_convert_fusion.1
  27.0 1.0 fusion.71
  28.0 2.1 fusion.4
  30.1 1.7 gather_fusion.5
  32.8 4.0 collective-permute-start.2
  37.5 1.3 collective-permute-start.3
  38.8 1.6 fusion.66
  40.4 1.7 collective-permute-done.3
  43.1 1.2 convolution_add_fusion.3
  44.3 1.0 fusion.61
  45.3 1.0 fusion.9
  47.9 1.6 gather_fusion
  51.5 76.6 %all-gather.3.cloned.1.call-done = bf16[1,1,4096,128]{2,3,0,1:T(8,128)(2,1)} async-done(((bf16[1,1,128,128]{2,3,0,1:T(8,128)(2,1)}), bf16[1,1,4096,128]{2,3,0,1:T(8,128)(2,1)}) %all-gather.3.cloned.1.call-update) | async-done | bytes 1048592 | tf_op jit(solution)/shard_map/all_gather | solution.py:147
  128.1 2.3 copy.94
  130.4 1.8 gather_fusion.10
  136.8 1.1 convolution_bitcast_fusion.7
  138.0 1.6 broadcast.143
  139.6 2.2 scatter_fusion
  141.8 2.9 copy.95
  147.3 218.4 %reduce-scatter.2.cloned.1.call-done = f32[1,128,128]{1,2,0:T(8,128)} async-done(((f32[1,4096,128]{1,2,0:T(8,128)}), f32[1,128,128]{1,2,0:T(8,128)}) %reduce-scatter.2.cloned.1.call-update) | async-done | bytes 65552 | tf_op jit(solution)/shard_map/reduce_scatter | solution.py:167
  365.8 1.2 convolution_bitcast_fusion.8
  368.4 1.2 fusion.10
  369.6 1.0 fusion.11
  370.6 0.9 convolution_convert_fusion.1
  371.6 1.2 convolution_bitcast_fusion.4
  372.8 1.4 copy.53
  374.2 1.4 scatter_fusion.2
  376.3 1.3 convolution_bitcast_fusion.13
  378.3 2.1 collective-permute-start.4
  380.5 1.3 collective-permute-start.5
  381.8 0.9 fusion.8
  382.8 1.5 scatter_custom_fusion.3
  384.3 2.2 collective-permute-done.5
  386.4 1.7 scatter_custom_fusion.4
  388.4 1.0 copy.55
  389.5 2.0 scatter_fusion.3
  391.6 1.2 bitcast_add_fusion
  392.9 1.1 convolution_bitcast_fusion.17
  394.1 1.4 fusion.5
  395.5 1.0 convolution_bitcast_fusion.18
  396.4 1.3 fusion.6
  397.8 1.0 convolution_bitcast_fusion.19
  398.7 1.0 convolution_bitcast_fusion.20
  399.7 1.0 convolution_convert_fusion
  400.8 2.3 convolution_bitcast_fusion.2
  403.0 3.6 copy.58
  406.7 6.7 scatter_fusion.4
  413.5 1.1 slice.158
  415.3 0.9 pad_maximum_fusion
  416.3 3.4 collective-permute-start.6
  419.6 1.3 collective-permute-start.7
  420.9 2.5 fusion.3
  423.5 3.5 scatter_custom_fusion.7
  426.9 3.5 scatter_custom_fusion.8
  430.4 2.1 convert_bitcast_fusion
  432.5 261.5 %all-reduce.2.cloned.1.call-done = f32[3,4,128,128]{2,3,1,0:T(8,128)} async-done(((f32[3,4,128,128]{2,3,1,0:T(8,128)}), f32[3,4,128,128]{2,3,1,0:T(8,128)}) %all-reduce.2.cloned.1.call-update) | async-done | bytes 786448 | tf_op jit(solution)/shard_map/psum | solution.py:198
  694.0 2.3 copy.70
  (180 shorter events, 19.6 us)
Async XLA Ops:
  7.2 15.5 %copy-start = (bf16[16,3,128,128]{3,2,1,0:T(8,128)(2,1)S(1)}, bf16[16,3,128,128]{3,2,1,0:T(8,128)(2,1)}, u32[]{:S(2)}) copy-start(bf16[16,3,128,128]{3,2,1,0:T(8,128)(2,1)} %param.18) | copy-start | bytes 4718596
  7.2 13.4 %copy-start.1 = (bf16[1,2048,128]{2,1,0:T(8,128)(2,1)S(1)}, bf16[1,2048,128]{2,1,0:T(8,128)(2,1)}, u32[]{:S(2)}) copy-start(bf16[1,2048,128]{2,1,0:T(8,128)(2,1)} %param.15) | copy-start | bytes 1572868
  7.2 13.0 %copy-start.33 = (s32[4,2]{0,1:T(2,128)S(1)}, s32[4,2]{0,1:T(2,128)}, u32[]{:S(2)}) copy-start(s32[4,2]{0,1:T(2,128)} %param.22) | copy-start | bytes 100
  7.2 13.2 %copy-start.39 = (s32[1,2,128]{2,1,0:T(2,128)S(1)}, s32[1,2,128]{2,1,0:T(2,128)}, u32[]{:S(2)}) copy-start(s32[1,2,128]{2,1,0:T(2,128)} %param.25) | copy-start | bytes 3076
  7.2 13.2 %copy-start.32 = (s32[4,3]{1,0:T(4,128)S(1)}, s32[4,3]{1,0:T(4,128)}, u32[]{:S(2)}) copy-start(s32[4,3]{1,0:T(4,128)} %param.24) | copy-start | bytes 148
  7.2 13.3 %copy-start.40 = (s32[1,2]{1,0:T(1,128)S(1)}, s32[1,2]{1,0:T(1,128)}, u32[]{:S(2)}) copy-start(s32[1,2]{1,0:T(1,128)} %param.27) | copy-start | bytes 28
  7.2 120.9 %all-gather.3.cloned.1.call-start = ((), (), s32[]{:S(2)}) async-start(), calls=%async_computation.3 | async-start | bytes 1081344 | tf_op jit(solution)/shard_map/all_gather | solution.py:147
  8.1 7.6 %copy-start.36 = (s32[128]{0:T(128)}, s32[128]{0:T(128)S(1)}, u32[]{:S(2)}) copy-start(s32[128]{0:T(128)S(1)} %get-tuple-element.13) | copy-start | bytes 1540
  8.1 8.9 %copy-start.35 = (s32[128]{0:T(128)}, s32[128]{0:T(128)S(1)}, u32[]{:S(2)}) copy-start(s32[128]{0:T(128)S(1)} %get-tuple-element.12) | copy-start | bytes 1540
  9.9 10.7 %collective-permute-start = (bf16[1,1,128,128]{3,2,1,0:T(8,128)(2,1)S(1)}, bf16[1,1,128,128]{3,2,1,0:T(8,128)(2,1)S(1)}, u32[]{:S(2)}, u32[]{:S(2)}) collective-permute-start(bf16[1,1,128,128]{3,2,1,0:T(8,128)(2,1)S(1)} %bitcast.434), channel_id=1, source_target_pairs={{0,1},{1,2},{2,3},{3,4},{4,5},{5,6},{6,7},{7,8},{8,9},{9,10},{10,1... | collective-permute-start | bytes 98312 | tf_op jit(solution)/shard_map/ppermute | solution.py:15
  15.7 4.9 collective-permute-start.1
  20.4 2.3 copy-start.37
  20.4 2.3 copy-start.38
  22.7 2.1 copy-start.15
  24.8 2.2 copy-start.6
  27.0 3.1 copy-start.8
  28.0 2.1 copy-start.13
  28.0 3.8 copy-start.4
  30.1 12.7 %copy-start.10 = (bf16[4,3,128,128]{3,2,1,0:T(8,128)(2,1)S(1)}, bf16[4,3,128,128]{3,2,1,0:T(8,128)(2,1)}, u32[]{:S(2)}) copy-start(bf16[4,3,128,128]{3,2,1,0:T(8,128)(2,1)} %param.23) | copy-start | bytes 1179652
  32.8 7.6 %collective-permute-start.2 = (bf16[1,1,128,128]{3,2,1,0:T(8,128)(2,1)S(1)}, bf16[1,1,128,128]{3,2,1,0:T(8,128)(2,1)S(1)}, u32[]{:S(2)}, u32[]{:S(2)}) collective-permute-start(bf16[1,1,128,128]{3,2,1,0:T(8,128)(2,1)S(1)} %bitcast.436), channel_id=1, source_target_pairs={{0,1},{1,2},{2,3},{3,4},{4,5},{5,6},{6,7},{7,8},{8,9},{9,10},{10,1... | collective-permute-start | bytes 98312 | tf_op jit(solution)/shard_map/ppermute | solution.py:15
  37.5 4.7 collective-permute-start.3
  43.1 3.3 copy-start.11
  43.1 3.9 copy-start.18
  44.3 3.5 copy-start.21
  45.3 1.1 copy-start.47
  45.3 5.0 copy-start.42
  47.8 2.8 copy-start.19
  47.8 318.0 %reduce-scatter.2.cloned.1.call-start = ((), (), s32[]{:S(2)}) async-start(), calls=%async_computation.1 | async-start | bytes 2162688 | tf_op jit(solution)/shard_map/reduce_scatter | solution.py:167
  49.7 82.4 %copy-start.20 = (bf16[1,3,128,128]{3,2,1,0:T(8,128)(2,1)S(1)}, bf16[1,3,128,128]{3,2,1,0:T(8,128)(2,1)}, u32[]{:S(2)}) copy-start(bf16[1,3,128,128]{3,2,1,0:T(8,128)(2,1)} %param.28) | copy-start | bytes 294916
  133.3 3.5 copy-start.28
  134.3 0.6 copy-start.43
  135.9 3.7 copy-start.45
  144.8 0.7 copy-start.34
  144.8 0.8 copy-start.31
  144.8 1.4 copy-start.29
  144.8 1.5 copy-start.46
  144.8 1.7 copy-start.44
  144.8 222.2 %copy-start.41 = (s32[1,2]{1,0:T(1,128)S(1)}, s32[1,2]{1,0:T(1,128)}, u32[]{:S(2)}) copy-start(s32[1,2]{1,0:T(1,128)} %param.27) | copy-start | bytes 28
  144.8 549.2 %all-reduce.2.cloned.1.call-start = ((), (), s32[]{:S(2)}) async-start(), calls=%async_computation.2 | async-start | bytes 1572864 | tf_op jit(solution)/shard_map/psum | solution.py:198
  367.6 2.0 copy-start.22
  367.7 2.9 copy-start.27
  369.6 4.6 copy-start.49
  375.6 2.0 copy-start.23
  375.6 2.0 copy-start.50
  375.6 2.2 copy-start.12
  376.3 5.5 copy-start.16
  377.9 10.3 %copy-start.5 = (bf16[4,2,128,128]{3,2,1,0:T(8,128)(2,1)S(1)}, bf16[4,2,128,128]{3,2,1,0:T(8,128)(2,1)}, u32[]{:S(2)}) copy-start(bf16[4,2,128,128]{3,2,1,0:T(8,128)(2,1)} %param.21) | copy-start | bytes 786436
  378.3 4.4 collective-permute-start.4
  380.5 6.0 collective-permute-start.5
  391.5 1.4 copy-start.14
  392.9 1.1 copy-start.2
  394.1 1.4 copy-start.9
  394.1 2.4 copy-start.48
  396.4 1.3 copy-start.7
  413.4 1.8 copy-start.24
  413.5 1.8 copy-start.25
  413.5 1.8 copy-start.26
  413.5 1.8 copy-start.30
  413.5 1.8 copy-start.17
  415.2 5.7 copy-start.3
  416.3 7.2 %collective-permute-start.6 = (f32[1,1,128,128]{3,2,1,0:T(8,128)}, f32[1,1,128,128]{3,2,1,0:T(8,128)S(1)}, u32[]{:S(2)}, u32[]{:S(2)}) collective-permute-start(f32[1,1,128,128]{3,2,1,0:T(8,128)} %get-tuple-element.7), channel_id=1, source_target_pairs={{0,1},{1,2},{2,3},{3,4},{4,5},{5,6},{6,7},{7,8},{8,9},{9,10},{10,1... | collective-permute-start | bytes 196616 | tf_op jit(solution)/shard_map/ppermute | solution.py:15
  419.6 7.3 %collective-permute-start.7 = (f32[1,1,128,128]{3,2,1,0:T(8,128)}, f32[1,1,128,128]{3,2,1,0:T(8,128)S(1)}, u32[]{:S(2)}, u32[]{:S(2)}) collective-permute-start(f32[1,1,128,128]{3,2,1,0:T(8,128)} %get-tuple-element.6), channel_id=1, source_target_pairs={{1,0},{2,1},{3,2},{4,3},{5,4},{6,5},{7,6},{8,7},{9,8},{10,9},{11,1... | collective-permute-start | bytes 196616 | tf_op jit(solution)/shard_map/ppermute | solution.py:17
Sparse Core Ops, SparseCore 0:
  47.9 80.1 all-gather.2
  144.9 220.7 reduce-scatter.1
  416.4 277.5 all-reduce.1
where the time goes:
time: 705 us; the launch traced here: 703 us
  waiting for transfers between devices  560 us (79%)
  matrix products  44.1 us (6%)
  local copies, waits for them, and re-layouts  33.9 us (5%)
  other arithmetic  30.6 us (4%)
  starting transfers between devices  18.8 us (3%)
  between operations  14.9 us (2%)
    psum x1, waiting for transfers between devices, on_device(): weight_grad = lax.psum(weight_grad, ('dp', 'dom'))  262 us
    reduce_scatter x1, waiting for transfers between devices, on_device(): lax.psum_scatter(spread_top.reshape(snaps, -1, width), 'dom', scatter_dim...  218 us
    all_gather x1, waiting for transfers between devices, on_device(): every_top = lax.all_gather(top_in, 'dom', axis=1, tiled=True)  76.6 us
    dot_general x11, matrix products, mixed(): jnp.einsum('srw,wv->srv', left, right, preferred_element_type=jnp.float32)  15.3 us
  transfers between devices with their start and end apart: 11, of which 5 were waited for; matrix products, arithmetic and copies ran while one was open for 4% of the time, Pallas kernels for 0%

commit v1 on v0

v1 whole, which is shorter than its diff:
```python
import jax
import jax.numpy as jnp
from jax import lax
from jax.experimental import pallas as pl
from jax.experimental.pallas import tpu as pltpu
from jax.sharding import PartitionSpec as P

NY = 8
T = 128
FB, MB, TB = 16, 4, 1
GROUP = 4
F32, BF16 = jnp.float32, jnp.bfloat16
MESH = pl.DeviceIdType.MESH


def dot(a, b):
    return jnp.dot(a, b, preferred_element_type=F32)


def dot_bt(a, b):
    return lax.dot_general(a, b, (((1,), (1,)), ((), ())), preferred_element_type=F32)


def dot_at(a, b):
    return lax.dot_general(a, b, (((0,), (0,)), ((), ())), preferred_element_type=F32)


def logistic(s):
    return 0.5 * jnp.tanh(0.5 * s) + 0.5


def slope(s):
    q = logistic(s)
    return q * (1.0 + s * (1.0 - q))


def flat(blocks):
    return blocks.reshape(-1, T)


def tiled(rows):
    return rows.reshape(-1, T, T)


def picked_rows(export, source):
    columns = [
        jnp.transpose(jnp.broadcast_to(export[i : i + 1].astype(F32), (T, T))) for i in range(2)
    ]
    lane = lax.broadcasted_iota(jnp.int32, (T, T), 1).astype(F32)
    total = jnp.zeros((2 * T, T), F32)
    for pair in range(source.shape[0] // 2):
        onehot = jnp.concatenate(
            [
                jnp.concatenate(
                    [
                        jnp.where(column - T * (2 * pair + half) == lane, 1.0, 0.0)
                        for half in range(2)
                    ],
                    axis=1,
                )
                for column in columns
            ],
            axis=0,
        ).astype(BF16)
        total = total + dot(onehot, flat(source[2 * pair : 2 * pair + 2]))
    return tiled(total.astype(BF16))


def placed_rows(export, block, rows):
    row = lax.broadcasted_iota(jnp.int32, (T, T), 0) + block * T
    onehot = jnp.concatenate(
        [jnp.where(export[i : i + 1] == row, 1.0, 0.0) for i in range(2)], axis=1
    ).astype(BF16)
    return dot(onehot, rows)


def link(column, number, targets, prev, last):
    def before(s, carry):
        mine = column(s)
        best = jnp.int32(-1)
        for t in range(number):
            best = jnp.where((column(t) == mine) & (t < s), t, best)
        prev[s] = best
        return carry

    def final(j, carry):
        best = jnp.int32(-1)
        for t in range(number):
            best = jnp.where(column(t) == j, t, best)
        last[j] = best
        return carry

    lax.fori_loop(0, number, before, 0)
    lax.fori_loop(0, targets, final, 0)


def linked(pieces, at):
    return jnp.where(at >= 0, 1.0, 0.0) * pieces[jnp.maximum(at, 0)]


def chain(pieces, prev, number):
    def step(s, carry):
        pieces[s] = pieces[s] + linked(pieces, prev[s])
        return carry

    lax.fori_loop(0, number, step, 0)


def kernel(
    nx,
    ndp,
    nodes,
    cotangent,
    weights,
    fine_tiles,
    fcols,
    fexport,
    pool_tiles,
    pcols,
    mid_tiles,
    mcols,
    mexport,
    upper_tiles,
    ucols,
    top_tiles,
    tcols,
    node_grad,
    weight_grad,
    S,
    COT,
    M,
    FT,
    PT,
    MT,
    UT,
    TT,
    PART,
    PRE1,
    PRE2,
    ACT1,
    ACT2,
    MSG,
    OUT,
    GN,
    GM,
    PIECE,
    MS,
    MPART,
    MPRE1,
    MPRE2,
    MACT1,
    MACT2,
    MMSG,
    MOUT,
    GRADM,
    GRADML,
    MGN,
    MGM,
    MPIECE,
    PPIECE,
    UPIECE,
    fprev,
    flast,
    mprev,
    mlast,
    pprev,
    plast,
    uprev,
    ulast,
    HALO_S,
    HALO_R,
    MHALO_S,
    MHALO_R,
    BACK_S,
    BACK_R,
    MBACK_S,
    MBACK_R,
    COL_S,
    COL_R,
    YG,
    PARTNER,
    SEL_S,
    SEL_R,
    P1_S,
    P1_R,
    P2_S,
    P2_R,
    PY_S,
    PY_R,
    WACC,
    W1_S,
    W1_R,
    W1_Y,
    W1_X,
    W1_O,
    W0_S,
    W0_R,
    W0_Y,
    W0_X,
    W0_O,
    WOUT,
    ONODE,
    load_sem,
    send_sem,
    recv_sem,
):
    ny = NY
    ndom = nx * ny
    dp = lax.axis_index("dp")
    dom = lax.axis_index("dom")
    x = lax.div(dom, ny)
    y = lax.rem(dom, ny)

    left = (dp, lax.rem(dom + ndom - 1, ndom))
    right = (dp, lax.rem(dom + 1, ndom))

    def at_x(i):
        return (dp, lax.rem(x + i, nx) * ny + y)

    def at_y(i):
        return (dp, x * ny + lax.rem(y + i, ny))

    def at_dp(i):
        return (lax.rem(dp + i, ndp), dom)

    partners = (
        [left, right]
        + [at_x(i) for i in range(1, nx)]
        + [at_y(i) for i in range(1, ny)]
        + [at_dp(i) for i in range(1, ndp)]
    )
    barrier = pltpu.get_barrier_semaphore()
    for partner in partners:
        pl.semaphore_signal(barrier, inc=1, device_id=partner, device_id_type=MESH)

    started = []

    def send(src, dst, device):
        number = len(started)
        copy = pltpu.make_async_remote_copy(
            src_ref=src,
            dst_ref=dst,
            send_sem=send_sem.at[number],
            recv_sem=recv_sem.at[number],
            device_id=device,
            device_id_type=MESH,
        )
        copy.start()
        started.append(copy)
        return copy

    loads = []

    def load(src, dst):
        copy = pltpu.make_async_copy(src, dst, load_sem.at[len(loads)])
        copy.start()
        loads.append(copy)
        return copy

    got_nodes = load(nodes, S.at[pl.ds(0, FB)])
    got_cot = load(cotangent, COT)
    got_pool = load(pool_tiles, PT)
    got_upper = load(upper_tiles, UT)
    got_weights = load(weights, M)
    got_fine = load(fine_tiles, FT)
    got_mid = load(mid_tiles, MT)
    got_top = load(top_tiles, TT)

    has_left = jnp.where(dom > 0, 1.0, 0.0).astype(F32)
    has_right = jnp.where(dom < ndom - 1, 1.0, 0.0).astype(F32)

    def level(l):
        return [M[l, i] for i in range(4)]

    my_col = tcols[0, 2]
    COL_S[...] = jnp.full((8, T), my_col, jnp.int32)
    got_nodes.wait()
    HALO_S[...] = picked_rows(fexport[0], S)
    pl.semaphore_wait(barrier, len(partners))
    halo = [send(HALO_S.at[1], HALO_R.at[0], right), send(HALO_S.at[0], HALO_R.at[1], left)]
    cols_sent = [send(COL_S, COL_R.at[i - 1], at_x(i)) for i in range(1, nx)]

    got_cot.wait()
    got_pool.wait()
    got_upper.wait()
    for m in range(MB):
        pooled = dot(PT[m, 0], COT[pcols[m, 0]]) + dot(PT[m, 1], COT[pcols[m, 1]])
        GRADM[m] = pooled
        GRADML[m] = pooled.astype(BF16)
    grad_top = dot(UT[0, 0], GRADML[ucols[0, 0]]) + dot(UT[0, 1], GRADML[ucols[0, 1]])
    got_weights.wait()
    got_fine.wait()

    def fine_own(g, carry):
        base = g * GROUP
        m0 = M[0, 0]
        u = flat(S[pl.ds(base, GROUP)])
        PRE1[pl.ds(base, GROUP)] = tiled(dot(u, m0))
        for b in range(GROUP):
            PART[base + b] = dot(FT[base + b, 0], S[base + b])
        return carry

    lax.fori_loop(0, FB // GROUP, fine_own, 0)

    for copy in halo:
        copy.wait_recv()
    S[FB] = HALO_R[0] * has_left.astype(BF16)
    S[FB + 1] = HALO_R[1] * has_right.astype(BF16)

    def forward(u, v, own_pre, m):
        pre1 = own_pre + dot(v, m[1])
        act1 = (pre1 * logistic(pre1)).astype(BF16)
        pre2 = dot(act1, m[2])
        act2 = (pre2 * logistic(pre2)).astype(BF16)
        return pre1, act1, pre2, act2

    def fine_forward(g, carry):
        base = g * GROUP
        m = level(0)
        messages = []
        for b in range(GROUP):
            r = base + b
            messages.append(
                (
                    PART[r]
                    + dot(FT[r, 1], S[fcols[r, 1]])
                    + dot(FT[r, 2], S[fcols[r, 2]])
                ).astype(BF16)
            )
        v = jnp.concatenate(messages, axis=0)
        here = pl.ds(base, GROUP)
        u = flat(S[here])
        pre1, act1, pre2, act2 = forward(u, v, flat(PRE1[here]), m)
        MSG[here] = tiled(v)
        PRE1[here] = tiled(pre1)
        ACT1[here] = tiled(act1)
        PRE2[here] = tiled(pre2)
        ACT2[here] = tiled(act2)
        OUT[here] = tiled((u.astype(F32) + dot(act2, m[3])).astype(BF16))
        return carry

    lax.fori_loop(0, FB // GROUP, fine_forward, 0)

    for m in range(MB):
        MS[m] = (dot(PT[m, 0], OUT[pcols[m, 0]]) + dot(PT[m, 1], OUT[pcols[m, 1]])).astype(BF16)
    MHALO_S[...] = picked_rows(mexport[0], MS[0:MB])
    mid_halo = [send(MHALO_S.at[1], MHALO_R.at[0], right), send(MHALO_S.at[0], MHALO_R.at[1], left)]
    got_mid.wait()
    mm = level(1)
    mu = flat(MS[0:MB])
    MPRE1[...] = tiled(dot(mu, mm[0]))
    for r in range(MB):
        MPART[r] = dot(MT[r, 0], MS[r])
    got_top.wait()
    link(lambda s: ucols[0, s], 2, MB, uprev, ulast)
    for copy in mid_halo:
        copy.wait_recv()
    MS[MB] = MHALO_R[0] * has_left.astype(BF16)
    MS[MB + 1] = MHALO_R[1] * has_right.astype(BF16)
    mv = jnp.concatenate(
        [
            (
                MPART[r] + dot(MT[r, 1], MS[mcols[r, 1]]) + dot(MT[r, 2], MS[mcols[r, 2]])
            ).astype(BF16)
            for r in range(MB)
        ],
        axis=0,
    )
    pre1, act1, pre2, act2 = forward(mu, mv, flat(MPRE1[...]), mm)
    MOUT[...] = tiled((mu.astype(F32) + dot(act2, mm[3])).astype(BF16))
    top_in = (dot(UT[0, 0], MOUT[ucols[0, 0]]) + dot(UT[0, 1], MOUT[ucols[0, 1]])).astype(BF16)

    YG[0] = top_in
    along_y = [send(YG.at[0], YG.at[i], at_y(i)) for i in range(1, ny)]
    half = send(YG.at[0], PARTNER, at_x(nx // 2))
    MMSG[...] = tiled(mv)
    MACT1[...] = tiled(act1)
    MACT2[...] = tiled(act2)
    MPRE1[...] = tiled(slope(pre1))
    MPRE2[...] = tiled(slope(pre2))

    def fine_slopes(g, carry):
        here = pl.ds(g * 2, 2)
        PRE1[here] = slope(PRE1[here])
        PRE2[here] = slope(PRE2[here])
        return carry

    lax.fori_loop(0, FB // 2, fine_slopes, 0)
    tm = level(2)
    top_own = dot(top_in, tm[0])
    top_part = dot(TT[0, 0], top_in)
    for copy in cols_sent:
        copy.wait_recv()
    cols = [COL_S[0:1]] + [COL_R[i, 0:1] for i in range(nx - 1)]
    for copy in along_y:
        copy.wait_recv()

    def chosen(column):
        total = jnp.zeros((T, T), BF16)
        for k in range(ny):
            source = x * ny + lax.rem(y + ny - k, ny)
            total = total + jnp.where(column == source, 1.0, 0.0).astype(BF16) * YG[k]
        return total

    along_x = []
    for i in range(1, nx):
        SEL_S[i - 1] = chosen(cols[nx - i])
        along_x.append(send(SEL_S.at[i - 1], SEL_R.at[i - 1], at_x(i)))
    third = chosen(cols[0])
    half.wait_recv()
    top_part = top_part + dot(TT[0, 1], PARTNER[...])
    link(lambda s: pcols[lax.rem(s, MB), lax.div(s, MB)], 2 * MB, FB, pprev, plast)
    link(lambda s: mcols[lax.rem(s, MB), 1 + lax.div(s, MB)], 2 * MB, MB + 2, mprev, mlast)
    for copy in along_x:
        copy.wait_recv()
    for i in range(nx - 1):
        third = third + SEL_R[i]
    top_msg = (top_part + dot(TT[0, 2], third)).astype(BF16)
    pre1, act1, pre2, act2 = forward(top_in, top_msg, top_own, tm)

    def backward(g, slope1, slope2, m):
        gb = g.astype(BF16)
        gs = (dot_bt(gb, m[3]) * slope2).astype(BF16)
        gf = (dot_bt(gs, m[2]) * slope1).astype(BF16)
        return gb, gs, gf, dot_bt(gf, m[1]).astype(BF16)

    def terms(u, v, act1, act2, gb, gs, gf):
        return dot_at(u, gf), dot_at(v, gf), dot_at(act1, gs), dot_at(act2, gb)

    gb, gs, gf, gm = backward(grad_top, slope(pre1), slope(pre2), tm)
    P2_S[...] = dot_at(TT[0, 2], gm).astype(BF16)
    back_x = [send(P2_S, P2_R.at[i - 1], at_x(i)) for i in range(1, nx)]
    P1_S[...] = dot_at(TT[0, 1], gm).astype(BF16)
    back_half = send(P1_S, P1_R, at_x(nx // 2))
    grad_top_in = grad_top + dot_bt(gf, tm[0]) + dot_at(TT[0, 0], gm)
    for i, term in enumerate(terms(top_in, top_msg, act1, act2, gb, gs, gf)):
        W1_S[pl.ds((4 + i) * T, T)] = term.astype(BF16)
    for copy in back_x:
        copy.wait_recv()
    arrived = [P2_S[...].astype(F32)] + [P2_R[i].astype(F32) for i in range(nx - 1)]

    def summed(target):
        total = jnp.zeros((T, T), F32)
        for column, piece in zip(cols, arrived):
            total = total + jnp.where(column == target, 1.0, 0.0) * piece
        return total

    back_y = []
    for i in range(1, ny):
        PY_S[i - 1] = summed(x * ny + lax.rem(y + i, ny)).astype(BF16)
        back_y.append(send(PY_S.at[i - 1], PY_R.at[i - 1], at_y(i)))
    grad_top_in = grad_top_in + summed(dom)
    link(lambda s: fcols[lax.rem(s, FB), 1 + lax.div(s, FB)], 2 * FB, FB + 2, fprev, flast)
    back_half.wait_recv()
    grad_top_in = grad_top_in + P1_R[...].astype(F32)
    for copy in back_y:
        copy.wait_recv()
    for i in range(ny - 1):
        grad_top_in = grad_top_in + PY_R[i].astype(F32)

    low = grad_top_in.astype(BF16)
    for s in range(2):
        UPIECE[s] = dot_at(UT[0, s], low)
    chain(UPIECE, uprev, 2)
    for m in range(MB):
        GRADM[m] = GRADM[m] + linked(UPIECE, ulast[m])
    g = flat(GRADM[...])
    gb, gs, gf, gm = backward(g, flat(MPRE1[...]), flat(MPRE2[...]), mm)
    MGM[...] = tiled(gm)
    for r in range(MB):
        MPIECE[r] = dot_at(MT[r, 1], MGM[r])
        MPIECE[MB + r] = dot_at(MT[r, 2], MGM[r])
    chain(MPIECE, mprev, 2 * MB)
    MBACK_S[0] = linked(MPIECE, mlast[MB]).astype(BF16)
    MBACK_S[1] = linked(MPIECE, mlast[MB + 1]).astype(BF16)
    mid_back = [send(MBACK_S.at[1], MBACK_R.at[0], right), send(MBACK_S.at[0], MBACK_R.at[1], left)]
    MGN[...] = tiled(g + dot_bt(gf, mm[0]))
    for r in range(MB):
        MGN[r] = MGN[r] + dot_at(MT[r, 0], MGM[r]) + linked(MPIECE, mlast[r])
    for i, term in enumerate(
        terms(flat(MS[0:MB]), flat(MMSG[...]), flat(MACT1[...]), flat(MACT2[...]), gb, gs, gf)
    ):
        W1_S[pl.ds(i * T, T)] = term.astype(BF16)

    def scattered(store, slots, rows):
        return [
            send(
                store.at[pl.ds(pl.multiple_of(at_dp(i)[0] * rows, rows), rows)],
                slots.at[i - 1],
                at_dp(i),
            )
            for i in range(1, ndp)
        ]

    def chunk_sum(copies, store, slots, rows):
        for copy in copies:
            copy.wait_recv()
        total = store[pl.ds(pl.multiple_of(dp * rows, rows), rows)].astype(F32)
        for i in range(ndp - 1):
            total = total + slots[i].astype(F32)
        return total.astype(BF16)

    def spread_y(value, slots):
        slots[y] = value
        return [send(slots.at[y], slots.at[y], at_y(i)) for i in range(1, ny)]

    def spread_x(value, slots):
        slots[x] = value
        return [send(slots.at[x], slots.at[x], at_x(i)) for i in range(1, nx)]

    def slot_sum(copies, slots, number):
        for copy in copies:
            copy.wait_recv()
        total = slots[0].astype(F32)
        for i in range(1, number):
            total = total + slots[i].astype(F32)
        return total.astype(BF16)

    def gathered(value, store, rows):
        mine = pl.ds(pl.multiple_of(dp * rows, rows), rows)
        store[mine] = value
        return [send(store.at[mine], store.at[mine], at_dp(i)) for i in range(1, ndp)]

    rows1 = 8 * T // ndp
    rows0 = 4 * T // ndp
    w1 = scattered(W1_S, W1_R, rows1)

    for copy in mid_back:
        copy.wait_recv()
    back_rows = jnp.concatenate(
        [MBACK_R[0] * has_left.astype(BF16), MBACK_R[1] * has_right.astype(BF16)], axis=0
    )
    for r in range(MB):
        MGN[r] = MGN[r] + placed_rows(mexport[0], r, back_rows)
    for m in range(MB):
        low = MGN[m].astype(BF16)
        for k in range(2):
            PPIECE[k * MB + m] = dot_at(PT[m, k], low)
    chain(PPIECE, pprev, 2 * MB)

    WACC[...] = jnp.zeros_like(WACC)

    def fine_backward(g, carry):
        base = g * GROUP
        here = pl.ds(base, GROUP)
        m = level(0)
        grad = jnp.concatenate(
            [COT[base + b].astype(F32) + linked(PPIECE, plast[base + b]) for b in range(GROUP)],
            axis=0,
        )
        gb, gs, gf, gm = backward(grad, flat(PRE1[here]), flat(PRE2[here]), m)
        GM[here] = tiled(gm)
        GN[here] = tiled(grad + dot_bt(gf, m[0]))
        for i, term in enumerate(
            terms(flat(S[here]), flat(MSG[here]), flat(ACT1[here]), flat(ACT2[here]), gb, gs, gf)
        ):
            WACC[i] = WACC[i] + term
        return carry

    lax.fori_loop(0, FB // GROUP, fine_backward, 0)
    W0_S[...] = flat(WACC[...]).astype(BF16)
    w0 = scattered(W0_S, W0_R, rows0)
    w1 = spread_y(chunk_sum(w1, W1_S, W1_R, rows1), W1_Y)

    def fine_pieces(g, carry):
        for b in range(2):
            r = g * 2 + b
            grad = GM[r]
            PIECE[r] = dot_at(FT[r, 1], grad)
            PIECE[FB + r] = dot_at(FT[r, 2], grad)
            GN[r] = GN[r] + dot_at(FT[r, 0], grad)
        return carry

    lax.fori_loop(0, FB // 2, fine_pieces, 0)
    chain(PIECE, fprev, 2 * FB)
    BACK_S[0] = linked(PIECE, flast[FB]).astype(BF16)
    BACK_S[1] = linked(PIECE, flast[FB + 1]).astype(BF16)
    back = [send(BACK_S.at[1], BACK_R.at[0], right), send(BACK_S.at[0], BACK_R.at[1], left)]
    w0 = spread_y(chunk_sum(w0, W0_S, W0_R, rows0), W0_Y)
    w1 = spread_x(slot_sum(w1, W1_Y, ny), W1_X)
    for copy in back:
        copy.wait_recv()
    w0 = spread_x(slot_sum(w0, W0_Y, ny), W0_X)
    w1 = gathered(slot_sum(w1, W1_X, nx), W1_O, rows1)
    back_rows = jnp.concatenate(
        [BACK_R[0] * has_left.astype(BF16), BACK_R[1] * has_right.astype(BF16)], axis=0
    )
    fexp = fexport[0]

    def finish(r, carry):
        ONODE[r] = (
            GN[r] + linked(PIECE, flast[r]) + placed_rows(fexp, r, back_rows)
        ).astype(BF16)
        return carry

    w0 = gathered(slot_sum(w0, W0_X, nx), W0_O, rows0)
    lax.fori_loop(0, FB, finish, 0)
    put_nodes = load(ONODE, node_grad)
    for copy in w1:
        copy.wait_recv()
    WOUT[1:3] = W1_O[...].reshape(2, 4, T, T).astype(F32)
    for copy in w0:
        copy.wait_recv()
    WOUT[0] = W0_O[...].reshape(4, T, T).astype(F32)
    put_weights = load(WOUT, weight_grad)
    for copy in started:
        copy.wait_send()
    put_nodes.wait()
    put_weights.wait()


def on_device(nx, ndp, *args):
    (
        nodes,
        cotangent,
        weights,
        fine_tiles,
        fine_cols,
        fine_export,
        pool_tiles,
        pool_cols,
        mid_tiles,
        mid_cols,
        mid_export,
        top_pool_tiles,
        top_pool_cols,
        top_tiles,
        top_cols,
    ) = args
    ny = NY
    vmem, smem, anywhere = (
        pl.BlockSpec(memory_space=pltpu.VMEM),
        pl.BlockSpec(memory_space=pltpu.SMEM),
        pl.BlockSpec(memory_space=pl.ANY),
    )

    def low(*shape):
        return pltpu.VMEM(shape, BF16)

    def full(*shape):
        return pltpu.VMEM(shape, F32)

    def index(number):
        return pltpu.SMEM((number,), jnp.int32)

    rows1, rows0 = 8 * T // ndp, 4 * T // ndp
    copies = (
        4 * 2 + (nx - 1) * 3 + (ny - 1) * 2 + 2 + 2 * (2 * (ndp - 1) + (ny - 1) + (nx - 1))
    )
    scratch = [
        low(FB + 2, T, T),
        low(FB, T, T),
        low(3, 4, T, T),
        low(FB, 3, T, T),
        low(MB, 2, T, T),
        low(MB, 3, T, T),
        low(1, 2, T, T),
        low(1, 3, T, T),
        full(FB, T, T),
        full(FB, T, T),
        full(FB, T, T),
        low(FB, T, T),
        low(FB, T, T),
        low(FB, T, T),
        low(FB, T, T),
        full(FB, T, T),
        low(FB, T, T),
        full(2 * FB, T, T),
        low(MB + 2, T, T),
        full(MB, T, T),
        full(MB, T, T),
        full(MB, T, T),
        low(MB, T, T),
        low(MB, T, T),
        low(MB, T, T),
        low(MB, T, T),
        full(MB, T, T),
        low(MB, T, T),
        full(MB, T, T),
        low(MB, T, T),
        full(2 * MB, T, T),
        full(2 * MB, T, T),
        full(2, T, T),
        index(2 * FB),
        index(FB + 2),
        index(2 * MB),
        index(MB + 2),
        index(2 * MB),
        index(FB),
        index(2),
        index(MB),
        low(2, T, T),
        low(2, T, T),
        low(2, T, T),
        low(2, T, T),
        low(2, T, T),
        low(2, T, T),
        low(2, T, T),
        low(2, T, T),
        pltpu.VMEM((8, T), jnp.int32),
        pltpu.VMEM((nx - 1, 8, T), jnp.int32),
        low(ny, T, T),
        low(T, T),
        low(nx - 1, T, T),
        low(nx - 1, T, T),
        low(T, T),
        low(T, T),
        low(T, T),
        low(nx - 1, T, T),
        low(ny - 1, T, T),
        low(ny - 1, T, T),
        full(4, T, T),
        low(8 * T, T),
        low(ndp - 1, rows1, T),
        low(ny, rows1, T),
        low(nx, rows1, T),
        low(8 * T, T),
        low(4 * T, T),
        low(ndp - 1, rows0, T),
        low(ny, rows0, T),
        low(nx, rows0, T),
        low(4 * T, T),
        full(3, 4, T, T),
        low(FB, T, T),
        pltpu.SemaphoreType.DMA((10,)),
        pltpu.SemaphoreType.DMA((copies,)),
        pltpu.SemaphoreType.DMA((copies,)),
    ]

    def body(*refs):
        kernel(nx, ndp, *refs)

    node_grad, weight_grad = pl.pallas_call(
        body,
        out_shape=(
            jax.ShapeDtypeStruct((FB, T, T), BF16),
            jax.ShapeDtypeStruct((3, 4, T, T), F32),
        ),
        in_specs=[
            anywhere,
            anywhere,
            anywhere,
            anywhere,
            smem,
            vmem,
            anywhere,
            smem,
            anywhere,
            smem,
            vmem,
            anywhere,
            smem,
            anywhere,
            smem,
        ],
        out_specs=(anywhere, anywhere),
        scratch_shapes=scratch,
        compiler_params=pltpu.CompilerParams(
            collective_id=0, has_side_effects=True, vmem_limit_bytes=48 * 1024 * 1024
        ),
        name="mesh_step",
    )(
        nodes.reshape(FB, T, T),
        cotangent.reshape(FB, T, T),
        weights,
        fine_tiles,
        fine_cols,
        fine_export,
        pool_tiles,
        pool_cols,
        mid_tiles,
        mid_cols,
        mid_export,
        top_pool_tiles,
        top_pool_cols,
        top_tiles,
        top_cols,
    )
    return node_grad.reshape(nodes.shape), weight_grad


def solution(mesh):
    nx, ndp = mesh.shape["dom"] // NY, mesh.shape["dp"]

    def run(*args):
        return on_device(nx, ndp, *args)

    return jax.shard_map(
        run,
        mesh=mesh,
        in_specs=(
            P("dp", "dom", None),
            P("dp", "dom", None),
            P(),
            P("dom", None, None, None),
            P("dom", None),
            P("dom", None, None),
            P("dom", None, None, None),
            P("dom", None),
            P("dom", None, None, None),
            P("dom", None),
            P("dom", None, None),
            P("dom", None, None, None),
            P("dom", None),
            P("dom", None, None, None),
            P("dom", None),
        ),
        out_specs=(P("dp", "dom", None), P()),
        check_vma=False,
    )
```

time: 705 us -> 98.1 us (0.14)
  waiting for transfers between devices: 560 us -> 0 us
  Pallas kernels: 0 us -> 82.2 us
  matrix products: 44.1 us -> 0 us
  other arithmetic: 30.6 us -> 0 us
  local copies, waits for them, and re-layouts: 33.9 us -> 14.7 us
  starting transfers between devices: 18.8 us -> 0 us
  between operations: 14.9 us -> 0.65 us
    psum x1 -> x0, waiting for transfers between devices: 262 us -> none  [on_device(): weight_grad = lax.psum(weight_grad, ('dp', 'dom'))]
    reduce_scatter x1 -> x0, waiting for transfers between devices: 218 us -> none  [on_device(): lax.psum_scatter(spread_top.reshape(snaps, -1, width), 'dom', scatter_dim...]
    pallas_call x0 -> x1, Pallas kernels: none -> 82.2 us  [on_device(): pl.pallas_call(body, out_shape=(jax.ShapeDtypeStruct((FB, T, T), BF16), j...]
    all_gather x1 -> x0, waiting for transfers between devices: 76.6 us -> none  [on_device(): every_top = lax.all_gather(top_in, 'dom', axis=1, tiled=True)]
    dot_general x45 -> x0, matrix products: 44.1 us -> none  [the longest x11 15.3 us: mixed(): jnp.einsum('srw,wv->srv', left, right, preferred_element_type=jnp.float32)]
    scatter-add x9 -> x0, other arithmetic: 23.1 us -> none  [the longest x5 13 us: tile_spread(): summed = jax.ops.segment_sum(flat, columns.reshape(-1), num_segments=number)]
    ppermute x8 -> x0, starting transfers between devices: 18.7 us -> none  [the longest x4 13.5 us: extended_2(): lax.ppermute(tail, axis, [(i, (i + 1) % count) for i in range(ends)])]
    gather x11 -> x0, local copies, waits for them, and re-layouts: 13.8 us -> none  [the longest x7 8.84 us: tile_apply(): picked = blocks[:, columns]]
  transfers between devices with their start and end apart: 11 -> 0, of which waited for: 5 -> 0; matrix products, arithmetic and copies ran while one was open for 4% -> 0% of each run, Pallas kernels for 0% -> 0%
where the time goes in v1:
time: 98.1 us; the launch traced here: 97.5 us
  Pallas kernels  82.2 us (84%)
  local copies, waits for them, and re-layouts  14.7 us (15%)
    pallas_call x1, Pallas kernels, on_device(): pl.pallas_call(body, out_shape=(jax.ShapeDtypeStruct((FB, T, T), BF16), j...  82.2 us
    unnamed x30, local copies, waits for them, and re-layouts  14.7 us

profile of v1, /device:TPU:1, one launch (start us, length us, event | category | flops | bytes accessed | tf_op | source)
XLA Modules:
  0.0 97.5 jit_solution(10375333565124469424)
XLA Ops:
  0.6 0.8 copy.18.refs_7_
  1.4 0.8 copy.17.refs_4_
  2.2 0.0 copy-start
  2.2 1.4 %copy-done = bf16[16,3,128,128]{3,2,1,0:T(8,128)(2,1)S(1)} copy-done((bf16[16,3,128,128]{3,2,1,0:T(8,128)(2,1)S(1)}, bf16[16,3,128,128]{3,2,1,0:T(8,128)(2,1)}, u32[]{:S(2)}) %copy-start) | copy-done | bytes 1572888
  3.6 0.0 copy-start.1
  3.6 1.0 %copy-done.1 = bf16[1,2048,128]{2,1,0:T(8,128)(2,1)S(1)} copy-done((bf16[1,2048,128]{2,1,0:T(8,128)(2,1)S(1)}, bf16[1,2048,128]{2,1,0:T(8,128)(2,1)}, u32[]{:S(2)}) %copy-start.1) | copy-done | bytes 524312
  4.6 0.0 copy-start.2
  4.6 1.0 %copy-done.2 = bf16[1,2048,128]{2,1,0:T(8,128)(2,1)S(1)} copy-done((bf16[1,2048,128]{2,1,0:T(8,128)(2,1)S(1)}, bf16[1,2048,128]{2,1,0:T(8,128)(2,1)}, u32[]{:S(2)}) %copy-start.2) | copy-done | bytes 524312
  5.6 0.0 copy-start.3
  5.6 1.0 %copy-done.3 = bf16[3,4,128,128]{3,2,1,0:T(8,128)(2,1)S(1)} copy-done((bf16[3,4,128,128]{3,2,1,0:T(8,128)(2,1)S(1)}, bf16[3,4,128,128]{3,2,1,0:T(8,128)(2,1)}, u32[]{:S(2)}) %copy-start.3) | copy-done | bytes 393240
  6.6 0.0 copy-start.4
  6.6 1.0 %copy-done.4 = bf16[4,3,128,128]{3,2,1,0:T(8,128)(2,1)S(1)} copy-done((bf16[4,3,128,128]{3,2,1,0:T(8,128)(2,1)S(1)}, bf16[4,3,128,128]{3,2,1,0:T(8,128)(2,1)}, u32[]{:S(2)}) %copy-start.4) | copy-done | bytes 393240
  7.6 0.0 copy-start.5
  7.6 0.9 copy-done.5
  8.6 0.0 copy-start.6
  8.6 0.9 copy-done.6
  9.5 0.0 copy-start.7
  9.5 0.8 copy-done.7
  10.3 0.0 copy-start.8
  10.3 0.7 copy-done.8
  11.0 0.0 copy-start.9
  11.0 0.7 copy-done.9
  11.7 0.0 copy-start.10
  11.7 0.7 copy-done.10
  12.4 0.0 copy-start.11
  12.4 0.7 copy-done.11
  13.0 0.0 copy-start.12
  13.0 0.7 copy-done.12
  13.7 82.2 %mesh_step.1 = (bf16[16,128,128]{2,1,0:T(8,128)(2,1)S(1)}, f32[3,4,128,128]{3,2,1,0:T(8,128)S(1)}) custom-call(bf16[16,128,128]{2,1,0:T(8,128)(2,1)S(1)} %bitcast.3, bf16[16,128,128]{2,1,0:T(8,128)(2,1)S(1)} %bitcast.4, bf16[3,4,128,128]{3,2,1,0:T(8,128)(2,1)S(1)} %copy-done.3, bf16[16,3,128,128]{3,2,1,0:T(8,128)(2,1)S(1)} %copy-done, ...), custom_call_target="tpu_custom_call" | custom-call | tf_op jit(solution)/shard_map/mesh_step/pallas_call | solution.py:733
  95.9 0.8 copy.21
  96.6 0.9 copy.22
Async XLA Ops:
  2.2 1.4 %copy-start = (bf16[16,3,128,128]{3,2,1,0:T(8,128)(2,1)S(1)}, bf16[16,3,128,128]{3,2,1,0:T(8,128)(2,1)}, u32[]{:S(2)}) copy-start(bf16[16,3,128,128]{3,2,1,0:T(8,128)(2,1)} %refs_3_.1) | copy-start | bytes 4718596
  3.6 1.0 %copy-start.1 = (bf16[1,2048,128]{2,1,0:T(8,128)(2,1)S(1)}, bf16[1,2048,128]{2,1,0:T(8,128)(2,1)}, u32[]{:S(2)}) copy-start(bf16[1,2048,128]{2,1,0:T(8,128)(2,1)} %param.15) | copy-start | bytes 1572868
  4.6 1.0 %copy-start.2 = (bf16[1,2048,128]{2,1,0:T(8,128)(2,1)S(1)}, bf16[1,2048,128]{2,1,0:T(8,128)(2,1)}, u32[]{:S(2)}) copy-start(bf16[1,2048,128]{2,1,0:T(8,128)(2,1)} %param.16) | copy-start | bytes 1572868
  5.6 1.0 %copy-start.3 = (bf16[3,4,128,128]{3,2,1,0:T(8,128)(2,1)S(1)}, bf16[3,4,128,128]{3,2,1,0:T(8,128)(2,1)}, u32[]{:S(2)}) copy-start(bf16[3,4,128,128]{3,2,1,0:T(8,128)(2,1)} %refs_2_.1) | copy-start | bytes 1179652
  6.6 1.0 %copy-start.4 = (bf16[4,3,128,128]{3,2,1,0:T(8,128)(2,1)S(1)}, bf16[4,3,128,128]{3,2,1,0:T(8,128)(2,1)}, u32[]{:S(2)}) copy-start(bf16[4,3,128,128]{3,2,1,0:T(8,128)(2,1)} %refs_8_.1) | copy-start | bytes 1179652
  7.6 0.9 copy-start.5
  8.6 0.9 copy-start.6
  9.5 0.8 copy-start.7
  10.3 0.7 copy-start.8
  11.0 0.7 copy-start.9
  11.7 0.7 copy-start.10
  12.4 0.7 copy-start.11
  13.0 0.7 copy-start.12

commit v2 on v1

--- a/solution.py
+++ b/solution.py
@@ -113,19 +113,26 @@
     cotangent,
     weights,
     fine_tiles,
+    fine_cols,
+    fine_export,
+    pool_tiles,
+    pool_cols,
+    mid_tiles,
+    mid_cols,
+    mid_export,
+    upper_tiles,
+    upper_cols,
+    top_tiles,
+    top_cols,
+    node_grad,
+    weight_grad,
     fcols,
     fexport,
-    pool_tiles,
     pcols,
-    mid_tiles,
     mcols,
     mexport,
-    upper_tiles,
     ucols,
-    top_tiles,
     tcols,
-    node_grad,
-    weight_grad,
     S,
     COT,
     M,
@@ -198,7 +205,6 @@
     W0_Y,
     W0_X,
     W0_O,
-    WOUT,
     ONODE,
     load_sem,
     send_sem,
@@ -258,12 +264,19 @@
         return copy
 
     got_nodes = load(nodes, S.at[pl.ds(0, FB)])
+    got_export = load(fine_export, fexport)
+    got_tcols = load(top_cols, tcols)
+    got_pcols = load(pool_cols, pcols)
+    got_ucols = load(upper_cols, ucols)
     got_cot = load(cotangent, COT)
     got_pool = load(pool_tiles, PT)
     got_upper = load(upper_tiles, UT)
     got_weights = load(weights, M)
     got_fine = load(fine_tiles, FT)
+    got_fcols = load(fine_cols, fcols)
     got_mid = load(mid_tiles, MT)
+    got_mcols = load(mid_cols, mcols)
+    got_mexport = load(mid_export, mexport)
     got_top = load(top_tiles, TT)
 
     has_left = jnp.where(dom > 0, 1.0, 0.0).astype(F32)
@@ -272,24 +285,24 @@
     def level(l):
         return [M[l, i] for i in range(4)]
 
-    my_col = tcols[0, 2]
-    COL_S[...] = jnp.full((8, T), my_col, jnp.int32)
+    got_export.wait()
     got_nodes.wait()
     HALO_S[...] = picked_rows(fexport[0], S)
     pl.semaphore_wait(barrier, len(partners))
     halo = [send(HALO_S.at[1], HALO_R.at[0], right), send(HALO_S.at[0], HALO_R.at[1], left)]
+    got_tcols.wait()
+    COL_S[...] = jnp.full((8, T), tcols[0, 2], jnp.int32)
     cols_sent = [send(COL_S, COL_R.at[i - 1], at_x(i)) for i in range(1, nx)]
 
-    got_cot.wait()
-    got_pool.wait()
-    got_upper.wait()
+    for copy in (got_cot, got_pool, got_pcols, got_upper, got_ucols):
+        copy.wait()
     for m in range(MB):
-        pooled = dot(PT[m, 0], COT[pcols[m, 0]]) + dot(PT[m, 1], COT[pcols[m, 1]])
+        pooled = dot(PT[m, 0], COT[pcols[0, m]]) + dot(PT[m, 1], COT[pcols[1, m]])
         GRADM[m] = pooled
         GRADML[m] = pooled.astype(BF16)
     grad_top = dot(UT[0, 0], GRADML[ucols[0, 0]]) + dot(UT[0, 1], GRADML[ucols[0, 1]])
-    got_weights.wait()
-    got_fine.wait()
+    for copy in (got_weights, got_fine, got_fcols):
+        copy.wait()
 
     def fine_own(g, carry):
         base = g * GROUP
@@ -323,8 +336,8 @@
             messages.append(
                 (
                     PART[r]
-                    + dot(FT[r, 1], S[fcols[r, 1]])
-                    + dot(FT[r, 2], S[fcols[r, 2]])
+                    + dot(FT[r, 1], S[fcols[1, r]])
+                    + dot(FT[r, 2], S[fcols[2, r]])
                 ).astype(BF16)
             )
         v = jnp.concatenate(messages, axis=0)
@@ -342,10 +355,12 @@
     lax.fori_loop(0, FB // GROUP, fine_forward, 0)
 
     for m in range(MB):
-        MS[m] = (dot(PT[m, 0], OUT[pcols[m, 0]]) + dot(PT[m, 1], OUT[pcols[m, 1]])).astype(BF16)
+        MS[m] = (dot(PT[m, 0], OUT[pcols[0, m]]) + dot(PT[m, 1], OUT[pcols[1, m]])).astype(BF16)
+    got_mexport.wait()
     MHALO_S[...] = picked_rows(mexport[0], MS[0:MB])
     mid_halo = [send(MHALO_S.at[1], MHALO_R.at[0], right), send(MHALO_S.at[0], MHALO_R.at[1], left)]
     got_mid.wait()
+    got_mcols.wait()
     mm = level(1)
     mu = flat(MS[0:MB])
     MPRE1[...] = tiled(dot(mu, mm[0]))
@@ -409,7 +424,7 @@
     third = chosen(cols[0])
     half.wait_recv()
     top_part = top_part + dot(TT[0, 1], PARTNER[...])
-    link(lambda s: pcols[lax.rem(s, MB), lax.div(s, MB)], 2 * MB, FB, pprev, plast)
+    link(lambda s: pcols[lax.div(s, MB), lax.rem(s, MB)], 2 * MB, FB, pprev, plast)
     link(lambda s: mcols[lax.rem(s, MB), 1 + lax.div(s, MB)], 2 * MB, MB + 2, mprev, mlast)
     for copy in along_x:
         copy.wait_recv()
@@ -450,7 +465,7 @@
         PY_S[i - 1] = summed(x * ny + lax.rem(y + i, ny)).astype(BF16)
         back_y.append(send(PY_S.at[i - 1], PY_R.at[i - 1], at_y(i)))
     grad_top_in = grad_top_in + summed(dom)
-    link(lambda s: fcols[lax.rem(s, FB), 1 + lax.div(s, FB)], 2 * FB, FB + 2, fprev, flast)
+    link(lambda s: fcols[1 + lax.div(s, FB), lax.rem(s, FB)], 2 * FB, FB + 2, fprev, flast)
     back_half.wait_recv()
     grad_top_in = grad_top_in + P1_R[...].astype(F32)
     for copy in back_y:
@@ -598,15 +613,15 @@
     put_nodes = load(ONODE, node_grad)
     for copy in w1:
         copy.wait_recv()
-    WOUT[1:3] = W1_O[...].reshape(2, 4, T, T).astype(F32)
+    put_upper = load(W1_O, weight_grad.at[pl.ds(4 * T, 8 * T)])
     for copy in w0:
         copy.wait_recv()
-    WOUT[0] = W0_O[...].reshape(4, T, T).astype(F32)
-    put_weights = load(WOUT, weight_grad)
+    put_fine = load(W0_O, weight_grad.at[pl.ds(0, 4 * T)])
     for copy in started:
         copy.wait_send()
     put_nodes.wait()
-    put_weights.wait()
+    put_upper.wait()
+    put_fine.wait()
 
 
 def on_device(nx, ndp, *args):
@@ -628,11 +643,7 @@
         top_cols,
     ) = args
     ny = NY
-    vmem, smem, anywhere = (
-        pl.BlockSpec(memory_space=pltpu.VMEM),
-        pl.BlockSpec(memory_space=pltpu.SMEM),
-        pl.BlockSpec(memory_space=pl.ANY),
-    )
+    anywhere = pl.BlockSpec(memory_space=pl.ANY)
 
     def low(*shape):
         return pltpu.VMEM(shape, BF16)
@@ -648,6 +659,13 @@
         4 * 2 + (nx - 1) * 3 + (ny - 1) * 2 + 2 + 2 * (2 * (ndp - 1) + (ny - 1) + (nx - 1))
     )
     scratch = [
+        pltpu.SMEM((3, FB), jnp.int32),
+        pltpu.VMEM((1, 2, T), jnp.int32),
+        pltpu.SMEM((2, MB), jnp.int32),
+        pltpu.SMEM((MB, 3), jnp.int32),
+        pltpu.VMEM((1, 2, T), jnp.int32),
+        pltpu.SMEM((1, 2), jnp.int32),
+        pltpu.SMEM((1, 3), jnp.int32),
         low(FB + 2, T, T),
         low(FB, T, T),
         low(3, 4, T, T),
@@ -720,9 +738,8 @@
         low(ny, rows0, T),
         low(nx, rows0, T),
         low(4 * T, T),
-        full(3, 4, T, T),
         low(FB, T, T),
-        pltpu.SemaphoreType.DMA((10,)),
+        pltpu.SemaphoreType.DMA((20,)),
         pltpu.SemaphoreType.DMA((copies,)),
         pltpu.SemaphoreType.DMA((copies,)),
     ]
@@ -734,29 +751,13 @@
         body,
         out_shape=(
             jax.ShapeDtypeStruct((FB, T, T), BF16),
-            jax.ShapeDtypeStruct((3, 4, T, T), F32),
+            jax.ShapeDtypeStruct((12 * T, T), BF16),
         ),
-        in_specs=[
-            anywhere,
-            anywhere,
-            anywhere,
-            anywhere,
-            smem,
-            vmem,
-            anywhere,
-            smem,
-            anywhere,
-            smem,
-            vmem,
-            anywhere,
-            smem,
-            anywhere,
-            smem,
-        ],
+        in_specs=[anywhere] * 15,
         out_specs=(anywhere, anywhere),
         scratch_shapes=scratch,
         compiler_params=pltpu.CompilerParams(
-            collective_id=0, has_side_effects=True, vmem_limit_bytes=48 * 1024 * 1024
+            collective_id=0, has_side_effects=True, vmem_limit_bytes=64 * 1024 * 1024
         ),
         name="mesh_step",
     )(
@@ -764,10 +765,10 @@
         cotangent.reshape(FB, T, T),
         weights,
         fine_tiles,
-        fine_cols,
+        fine_cols.T,
         fine_export,
         pool_tiles,
-        pool_cols,
+        pool_cols.T,
         mid_tiles,
         mid_cols,
         mid_export,
@@ -776,7 +777,7 @@
         top_tiles,
         top_cols,
     )
-    return node_grad.reshape(nodes.shape), weight_grad
+    return node_grad.reshape(nodes.shape), weight_grad.reshape(weights.shape).astype(F32)
 
 
 def solution(mesh):

time: 98.1 us -> 86.7 us (0.88)
  local copies, waits for them, and re-layouts: 14.7 us -> 1.87 us
  other arithmetic: 0 us -> 1.95 us
    unnamed x30 -> x1, local copies, waits for them, and re-layouts: 14.7 us -> 1.87 us
    convert_element_type x0 -> x1, other arithmetic: none -> 1.95 us  [on_device(): weight_grad.reshape(weights.shape).astype(F32)]
where the time goes in v2:
time: 86.7 us; the launch traced here: 86.5 us
  Pallas kernels  82.1 us (95%)
  other arithmetic  1.95 us (2%)
  local copies, waits for them, and re-layouts  1.87 us (2%)
    pallas_call x1, Pallas kernels, on_device(): pl.pallas_call(body, out_shape=(jax.ShapeDtypeStruct((FB, T, T), BF16), j...  82.1 us
    convert_element_type x1, other arithmetic, on_device(): weight_grad.reshape(weights.shape).astype(F32)  1.95 us
    unnamed x1, local copies, waits for them, and re-layouts  1.87 us

profile of v2, /device:TPU:1, one launch (start us, length us, event | category | flops | bytes accessed | tf_op | source)
XLA Modules:
  0.0 86.5 jit_solution(8897727163750063102)
XLA Ops:
  0.6 82.1 %mesh_step.1 = (bf16[16,128,128]{2,1,0:T(8,128)(2,1)}, bf16[1536,128]{1,0:T(8,128)(2,1)}) custom-call(bf16[16,128,128]{2,1,0:T(8,128)(2,1)} %bitcast.8, bf16[16,128,128]{2,1,0:T(8,128)(2,1)} %bitcast.9, bf16[3,4,128,128]{3,2,1,0:T(8,128)(2,1)} %refs_2_.1, bf16[16,3,128,128]{3,2,1,0:T(8,128)(2,1)} %refs_3_.1, s32[3,16]{1,0:T(4,128)} %bitcast.11, ...), custom_call_target="tpu_custom_call" | custom-call | tf_op jit(solution)/shard_map/mesh_step/pallas_call | solution.py:750
  82.7 1.9 %convert.1 = f32[3,4,128,128]{3,2,1,0:T(8,128)} convert(bf16[3,4,128,128]{3,2,1,0:T(8,128)(2,1)} %bitcast.10) | non-fusion elementwise | flops 196608 | bytes 1179648 | tf_op jit(solution)/shard_map/convert_element_type | solution.py:780
  84.6 1.9 %copy.18 = bf16[1,2048,128]{2,1,0:T(8,128)(2,1)} copy(bf16[1,2048,128]{2,1,0:T(8,128)(2,1)} %bitcast.7) | data formatting | bytes 1048576

commit v3 on v2

--- a/solution.py
+++ b/solution.py
@@ -6,6 +6,7 @@
 from jax.sharding import PartitionSpec as P
 
 NY = 8
+NC = 2
 T = 128
 FB, MB, TB = 16, 4, 1
 GROUP = 4
@@ -32,6 +33,10 @@
 def slope(s):
     q = logistic(s)
     return q * (1.0 + s * (1.0 - q))
+
+
+def far_first(number):
+    return sorted(range(1, number), key=lambda i: -min(i, number - i))
 
 
 def flat(blocks):
@@ -195,16 +200,12 @@
     PY_S,
     PY_R,
     WACC,
-    W1_S,
-    W1_R,
-    W1_Y,
-    W1_X,
-    W1_O,
-    W0_S,
-    W0_R,
-    W0_Y,
-    W0_X,
-    W0_O,
+    W_S,
+    W_R,
+    W_Y,
+    W_Z,
+    W_O,
+    GF,
     ONODE,
     load_sem,
     send_sem,
@@ -216,6 +217,9 @@
     dom = lax.axis_index("dom")
     x = lax.div(dom, ny)
     y = lax.rem(dom, ny)
+    nz = ndp // NC
+    z = lax.div(dp, NC)
+    core = lax.rem(dp, NC)
 
     left = (dp, lax.rem(dom + ndom - 1, ndom))
     right = (dp, lax.rem(dom + 1, ndom))
@@ -226,14 +230,21 @@
     def at_y(i):
         return (dp, x * ny + lax.rem(y + i, ny))
 
-    def at_dp(i):
-        return (lax.rem(dp + i, ndp), dom)
-
+    def at_z(i):
+        return (lax.rem(z + i, nz) * NC + core, dom)
+
+    def at_cx(c, i):
+        return (z * NC + lax.rem(core + c, NC), lax.rem(x + i, nx) * ny + y)
+
+    x_order = far_first(nx)
+    y_order = far_first(ny)
+    z_order = far_first(nz)
+    cx_order = [(c, i) for c in range(NC) for i in range(nx) if (c, i) != (0, 0)]
     partners = (
         [left, right]
-        + [at_x(i) for i in range(1, nx)]
-        + [at_y(i) for i in range(1, ny)]
-        + [at_dp(i) for i in range(1, ndp)]
+        + [at_cx(c, i) for c, i in cx_order]
+        + [at_y(i) for i in y_order]
+        + [at_z(i) for i in z_order]
     )
     barrier = pltpu.get_barrier_semaphore()
     for partner in partners:
@@ -285,9 +296,49 @@
     def level(l):
         return [M[l, i] for i in range(4)]
 
+    rows = 4 * T // (NC * nx)
+
+    def chunk(c, i):
+        number = lax.rem(core + c, NC) * nx + lax.rem(x + i, nx)
+        return pl.ds(pl.multiple_of(number * rows, rows), rows)
+
+    def scattered(store, slots):
+        return [
+            send(store.at[chunk(c, i)], slots.at[n], at_cx(c, i))
+            for n, (c, i) in enumerate(cx_order)
+        ]
+
+    def scatter_sum(copies, store, slots):
+        for copy in copies:
+            copy.wait_recv()
+        total = store[chunk(0, 0)].astype(F32)
+        for n in range(len(cx_order)):
+            total = total + slots[n].astype(F32)
+        return total.astype(BF16)
+
+    def shown_y(value, slots):
+        slots[y] = value
+        return [send(slots.at[y], slots.at[y], at_y(i)) for i in y_order]
+
+    def shown_z(value, slots):
+        slots[z] = value
+        return [send(slots.at[z], slots.at[z], at_z(i)) for i in z_order]
+
+    def slot_sum(copies, slots, number):
+        for copy in copies:
+            copy.wait_recv()
+        total = slots[0].astype(F32)
+        for i in range(1, number):
+            total = total + slots[i].astype(F32)
+        return total.astype(BF16)
+
+    def gathered(store):
+        mine = store.at[chunk(0, 0)]
+        return [send(mine, mine, at_cx(c, i)) for c, i in cx_order]
+
     got_export.wait()
     got_nodes.wait()
-    HALO_S[...] = picked_rows(fexport[0], S)
+    HALO_S[...] = picked_rows(fexport[0], S.at[pl.ds(0, FB)])
     pl.semaphore_wait(barrier, len(partners))
     halo = [send(HALO_S.at[1], HALO_R.at[0], right), send(HALO_S.at[0], HALO_R.at[1], left)]
     got_tcols.wait()
@@ -386,7 +437,7 @@
     top_in = (dot(UT[0, 0], MOUT[ucols[0, 0]]) + dot(UT[0, 1], MOUT[ucols[0, 1]])).astype(BF16)
 
     YG[0] = top_in
-    along_y = [send(YG.at[0], YG.at[i], at_y(i)) for i in range(1, ny)]
+    along_y = [send(YG.at[0], YG.at[i], at_y(i)) for i in y_order]
     half = send(YG.at[0], PARTNER, at_x(nx // 2))
     MMSG[...] = tiled(mv)
     MACT1[...] = tiled(act1)
@@ -418,7 +469,7 @@
         return total
 
     along_x = []
-    for i in range(1, nx):
+    for i in x_order:
         SEL_S[i - 1] = chosen(cols[nx - i])
         along_x.append(send(SEL_S.at[i - 1], SEL_R.at[i - 1], at_x(i)))
     third = chosen(cols[0])
@@ -433,10 +484,14 @@
     top_msg = (top_part + dot(TT[0, 2], third)).astype(BF16)
     pre1, act1, pre2, act2 = forward(top_in, top_msg, top_own, tm)
 
-    def backward(g, slope1, slope2, m):
+    def back_to_first(g, slope1, slope2, m):
         gb = g.astype(BF16)
         gs = (dot_bt(gb, m[3]) * slope2).astype(BF16)
         gf = (dot_bt(gs, m[2]) * slope1).astype(BF16)
+        return gb, gs, gf
+
+    def backward(g, slope1, slope2, m):
+        gb, gs, gf = back_to_first(g, slope1, slope2, m)
         return gb, gs, gf, dot_bt(gf, m[1]).astype(BF16)
 
     def terms(u, v, act1, act2, gb, gs, gf):
@@ -444,12 +499,12 @@
 
     gb, gs, gf, gm = backward(grad_top, slope(pre1), slope(pre2), tm)
     P2_S[...] = dot_at(TT[0, 2], gm).astype(BF16)
-    back_x = [send(P2_S, P2_R.at[i - 1], at_x(i)) for i in range(1, nx)]
+    back_x = [send(P2_S, P2_R.at[i - 1], at_x(i)) for i in x_order]
     P1_S[...] = dot_at(TT[0, 1], gm).astype(BF16)
     back_half = send(P1_S, P1_R, at_x(nx // 2))
     grad_top_in = grad_top + dot_bt(gf, tm[0]) + dot_at(TT[0, 0], gm)
     for i, term in enumerate(terms(top_in, top_msg, act1, act2, gb, gs, gf)):
-        W1_S[pl.ds((4 + i) * T, T)] = term.astype(BF16)
+        W_S[2, pl.ds(i * T, T)] = term.astype(BF16)
     for copy in back_x:
         copy.wait_recv()
     arrived = [P2_S[...].astype(F32)] + [P2_R[i].astype(F32) for i in range(nx - 1)]
@@ -461,9 +516,10 @@
         return total
 
     back_y = []
-    for i in range(1, ny):
+    for i in y_order:
         PY_S[i - 1] = summed(x * ny + lax.rem(y + i, ny)).astype(BF16)
         back_y.append(send(PY_S.at[i - 1], PY_R.at[i - 1], at_y(i)))
+    top_sum = scattered(W_S.at[2], W_R.at[2])
     grad_top_in = grad_top_in + summed(dom)
     link(lambda s: fcols[1 + lax.div(s, FB), lax.rem(s, FB)], 2 * FB, FB + 2, fprev, flast)
     back_half.wait_recv()
@@ -472,6 +528,8 @@
         copy.wait_recv()
     for i in range(ny - 1):
         grad_top_in = grad_top_in + PY_R[i].astype(F32)
+
+    top_sum = shown_z(scatter_sum(top_sum, W_S.at[2], W_R.at[2]), W_Z.at[2])
 
     low = grad_top_in.astype(BF16)
     for s in range(2):
@@ -495,50 +553,9 @@
     for i, term in enumerate(
         terms(flat(MS[0:MB]), flat(MMSG[...]), flat(MACT1[...]), flat(MACT2[...]), gb, gs, gf)
     ):
-        W1_S[pl.ds(i * T, T)] = term.astype(BF16)
-
-    def scattered(store, slots, rows):
-        return [
-            send(
-                store.at[pl.ds(pl.multiple_of(at_dp(i)[0] * rows, rows), rows)],
-                slots.at[i - 1],
-                at_dp(i),
-            )
-            for i in range(1, ndp)
-        ]
-
-    def chunk_sum(copies, store, slots, rows):
-        for copy in copies:
-            copy.wait_recv()
-        total = store[pl.ds(pl.multiple_of(dp * rows, rows), rows)].astype(F32)
-        for i in range(ndp - 1):
-            total = total + slots[i].astype(F32)
-        return total.astype(BF16)
-
-    def spread_y(value, slots):
-        slots[y] = value
-        return [send(slots.at[y], slots.at[y], at_y(i)) for i in range(1, ny)]
-
-    def spread_x(value, slots):
-        slots[x] = value
-        return [send(slots.at[x], slots.at[x], at_x(i)) for i in range(1, nx)]
-
-    def slot_sum(copies, slots, number):
-        for copy in copies:
-            copy.wait_recv()
-        total = slots[0].astype(F32)
-        for i in range(1, number):
-            total = total + slots[i].astype(F32)
-        return total.astype(BF16)
-
-    def gathered(value, store, rows):
-        mine = pl.ds(pl.multiple_of(dp * rows, rows), rows)
-        store[mine] = value
-        return [send(store.at[mine], store.at[mine], at_dp(i)) for i in range(1, ndp)]
-
-    rows1 = 8 * T // ndp
-    rows0 = 4 * T // ndp
-    w1 = scattered(W1_S, W1_R, rows1)
+        W_S[1, pl.ds(i * T, T)] = term.astype(BF16)
+
+    mid_sum = scattered(W_S.at[1], W_R.at[1])
 
     for copy in mid_back:
         copy.wait_recv()
@@ -553,6 +570,8 @@
             PPIECE[k * MB + m] = dot_at(PT[m, k], low)
     chain(PPIECE, pprev, 2 * MB)
 
+    top_sum = shown_y(slot_sum(top_sum, W_Z.at[2], nz), W_Y.at[2])
+
     WACC[...] = jnp.zeros_like(WACC)
 
     def fine_backward(g, carry):
@@ -563,9 +582,9 @@
             [COT[base + b].astype(F32) + linked(PPIECE, plast[base + b]) for b in range(GROUP)],
             axis=0,
         )
-        gb, gs, gf, gm = backward(grad, flat(PRE1[here]), flat(PRE2[here]), m)
-        GM[here] = tiled(gm)
-        GN[here] = tiled(grad + dot_bt(gf, m[0]))
+        gb, gs, gf = back_to_first(grad, flat(PRE1[here]), flat(PRE2[here]), m)
+        GN[here] = tiled(grad)
+        GF[here] = tiled(gf)
         for i, term in enumerate(
             terms(flat(S[here]), flat(MSG[here]), flat(ACT1[here]), flat(ACT2[here]), gb, gs, gf)
         ):
@@ -573,9 +592,18 @@
         return carry
 
     lax.fori_loop(0, FB // GROUP, fine_backward, 0)
-    W0_S[...] = flat(WACC[...]).astype(BF16)
-    w0 = scattered(W0_S, W0_R, rows0)
-    w1 = spread_y(chunk_sum(w1, W1_S, W1_R, rows1), W1_Y)
+    W_S[0] = flat(WACC[...]).astype(BF16)
+    fine_sum = scattered(W_S.at[0], W_R.at[0])
+    mid_sum = shown_y(scatter_sum(mid_sum, W_S.at[1], W_R.at[1]), W_Y.at[1])
+
+    def fine_rows(g, carry):
+        here = pl.ds(g * GROUP, GROUP)
+        gf = flat(GF[here])
+        GM[here] = tiled(dot_bt(gf, M[0, 1]).astype(BF16))
+        GN[here] = GN[here] + tiled(dot_bt(gf, M[0, 0]))
+        return carry
+
+    lax.fori_loop(0, FB // GROUP, fine_rows, 0)
 
     def fine_pieces(g, carry):
         for b in range(2):
@@ -591,12 +619,17 @@
     BACK_S[0] = linked(PIECE, flast[FB]).astype(BF16)
     BACK_S[1] = linked(PIECE, flast[FB + 1]).astype(BF16)
     back = [send(BACK_S.at[1], BACK_R.at[0], right), send(BACK_S.at[0], BACK_R.at[1], left)]
-    w0 = spread_y(chunk_sum(w0, W0_S, W0_R, rows0), W0_Y)
-    w1 = spread_x(slot_sum(w1, W1_Y, ny), W1_X)
+
+    half = rows // 2
+    value = scatter_sum(fine_sum, W_S.at[0], W_R.at[0])
+    first = shown_y(value[0:half], W_Y.at[0, :, 0:half])
+    second = shown_z(value[half:rows], W_Z.at[0, :, half:rows])
+    mid_sum = shown_z(slot_sum(mid_sum, W_Y.at[1], ny), W_Z.at[1])
+    W_O[2, chunk(0, 0)] = slot_sum(top_sum, W_Y.at[2], ny)
+    top_sum = gathered(W_O.at[2])
+
     for copy in back:
         copy.wait_recv()
-    w0 = spread_x(slot_sum(w0, W0_Y, ny), W0_X)
-    w1 = gathered(slot_sum(w1, W1_X, nx), W1_O, rows1)
     back_rows = jnp.concatenate(
         [BACK_R[0] * has_left.astype(BF16), BACK_R[1] * has_right.astype(BF16)], axis=0
     )
@@ -608,20 +641,68 @@
         ).astype(BF16)
         return carry
 
-    w0 = gathered(slot_sum(w0, W0_X, nx), W0_O, rows0)
-    lax.fori_loop(0, FB, finish, 0)
+    lax.fori_loop(0, FB // 2, finish, 0)
+    first = shown_z(slot_sum(first, W_Y.at[0, :, 0:half], ny), W_Z.at[0, :, 0:half])
+    second = shown_y(slot_sum(second, W_Z.at[0, :, half:rows], nz), W_Y.at[0, :, half:rows])
+    W_O[1, chunk(0, 0)] = slot_sum(mid_sum, W_Z.at[1], nz)
+    mid_sum = gathered(W_O.at[1])
+    lax.fori_loop(FB // 2, FB, finish, 0)
     put_nodes = load(ONODE, node_grad)
-    for copy in w1:
-        copy.wait_recv()
-    put_upper = load(W1_O, weight_grad.at[pl.ds(4 * T, 8 * T)])
-    for copy in w0:
-        copy.wait_recv()
-    put_fine = load(W0_O, weight_grad.at[pl.ds(0, 4 * T)])
+    W_O[0, chunk(0, 0)] = jnp.concatenate(
+        [
+            slot_sum(first, W_Z.at[0, :, 0:half], nz),
+            slot_sum(second, W_Y.at[0, :, half:rows], ny),
+        ],
+        axis=0,
+    )
+    fine_sum = gathered(W_O.at[0])
+    for copy in top_sum + mid_sum:
+        copy.wait_recv()
+    put_upper = load(W_O.at[pl.ds(1, 2)], weight_grad.at[pl.ds(1, 2)])
+    for copy in fine_sum:
+        copy.wait_recv()
+    put_fine = load(W_O.at[0], weight_grad.at[0])
     for copy in started:
         copy.wait_send()
     put_nodes.wait()
     put_upper.wait()
     put_fine.wait()
+
+
+def write_kernel(node_in, weight_in, node_out, weight_out, low, full, sem):
+    nodes = pltpu.make_async_copy(node_in, node_out, sem.at[0])
+    nodes.start()
+    fetch = [pltpu.make_async_copy(weight_in.at[l], low.at[l], sem.at[1 + l]) for l in range(3)]
+    put = [pltpu.make_async_copy(full.at[l], weight_out.at[l], sem.at[4 + l]) for l in range(3)]
+    for copy in fetch:
+        copy.start()
+    for l in range(3):
+        fetch[l].wait()
+        full[l] = low[l].astype(F32)
+        put[l].start()
+    for copy in put:
+        copy.wait()
+    nodes.wait()
+
+
+def written(node_grad, weight_grad):
+    anywhere = pl.BlockSpec(memory_space=pl.ANY)
+    return pl.pallas_call(
+        write_kernel,
+        out_shape=(
+            jax.ShapeDtypeStruct(node_grad.shape, BF16),
+            jax.ShapeDtypeStruct(weight_grad.shape, F32),
+        ),
+        in_specs=[anywhere] * 2,
+        out_specs=(anywhere, anywhere),
+        scratch_shapes=[
+            pltpu.VMEM(weight_grad.shape, BF16),
+            pltpu.VMEM(weight_grad.shape, F32),
+            pltpu.SemaphoreType.DMA((7,)),
+        ],
+        compiler_params=pltpu.CompilerParams(vmem_limit_bytes=64 * 1024 * 1024),
+        name="write_results",
+    )(node_grad, weight_grad)
 
 
 def on_device(nx, ndp, *args):
@@ -654,9 +735,15 @@
     def index(number):
         return pltpu.SMEM((number,), jnp.int32)
 
-    rows1, rows0 = 8 * T // ndp, 4 * T // ndp
+    nz = ndp // NC
+    rows = 4 * T // (NC * nx)
     copies = (
-        4 * 2 + (nx - 1) * 3 + (ny - 1) * 2 + 2 + 2 * (2 * (ndp - 1) + (ny - 1) + (nx - 1))
+        4 * 2
+        + (nx - 1) * 3
+        + (ny - 1) * 2
+        + 2
+        + 3 * 2 * (NC * nx - 1)
+        + 4 * (ny - 1 + nz - 1)
     )
     scratch = [
         pltpu.SMEM((3, FB), jnp.int32),
@@ -728,16 +815,12 @@
         low(ny - 1, T, T),
         low(ny - 1, T, T),
         full(4, T, T),
-        low(8 * T, T),
-        low(ndp - 1, rows1, T),
-        low(ny, rows1, T),
-        low(nx, rows1, T),
-        low(8 * T, T),
-        low(4 * T, T),
-        low(ndp - 1, rows0, T),
-        low(ny, rows0, T),
-        low(nx, rows0, T),
-        low(4 * T, T),
+        low(3, 4 * T, T),
+        low(3, NC * nx - 1, rows, T),
+        low(3, ny, rows, T),
+        low(3, nz, rows, T),
+        low(3, 4 * T, T),
+        low(FB, T, T),
         low(FB, T, T),
         pltpu.SemaphoreType.DMA((20,)),
         pltpu.SemaphoreType.DMA((copies,)),
@@ -751,7 +834,7 @@
         body,
         out_shape=(
             jax.ShapeDtypeStruct((FB, T, T), BF16),
-            jax.ShapeDtypeStruct((12 * T, T), BF16),
+            jax.ShapeDtypeStruct((3, 4 * T, T), BF16),
         ),
         in_specs=[anywhere] * 15,
         out_specs=(anywhere, anywhere),
@@ -777,7 +860,8 @@
         top_tiles,
         top_cols,
     )
-    return node_grad.reshape(nodes.shape), weight_grad.reshape(weights.shape).astype(F32)
+    node_grad, weight_grad = written(node_grad, weight_grad)
+    return node_grad.reshape(nodes.shape), weight_grad.reshape(weights.shape)
 
 
 def solution(mesh):

time: 86.7 us -> 94.7 us (1.092)
  Pallas kernels: 82.1 us -> 93.9 us
  other arithmetic: 1.95 us -> 0 us
  local copies, waits for them, and re-layouts: 1.87 us -> 0 us
    pallas_call x0 -> x1, Pallas kernels: none -> 17 us  [written(): pl.pallas_call(write_kernel, out_shape=(jax.ShapeDtypeStruct(node_grad.sh...]
    pallas_call x1, Pallas kernels: 82.1 us -> 76.8 us  [on_device(): pl.pallas_call(body, out_shape=(jax.ShapeDtypeStruct((FB, T, T), BF16), j...]
    convert_element_type x1 -> x0, other arithmetic: 1.95 us -> none  [on_device(): weight_grad.reshape(weights.shape).astype(F32)]
    unnamed x1 -> x0, local copies, waits for them, and re-layouts: 1.87 us -> none
where the time goes in v3:
time: 94.7 us; the launch traced here: 94.5 us
  Pallas kernels  93.9 us (99%)
    pallas_call x1, Pallas kernels, on_device(): pl.pallas_call(body, out_shape=(jax.ShapeDtypeStruct((FB, T, T), BF16), j...  76.8 us
    pallas_call x1, Pallas kernels, written(): pl.pallas_call(write_kernel, out_shape=(jax.ShapeDtypeStruct(node_grad.sh...  17 us

profile of v3, /device:TPU:1, one launch (start us, length us, event | category | flops | bytes accessed | tf_op | source)
XLA Modules:
  0.0 94.5 jit_solution(13617498015651868202)
XLA Ops:
  0.6 76.8 %mesh_step.1 = (bf16[16,128,128]{2,1,0:T(8,128)(2,1)}, bf16[3,512,128]{2,1,0:T(8,128)(2,1)}) custom-call(bf16[16,128,128]{2,1,0:T(8,128)(2,1)} %bitcast.6, bf16[16,128,128]{2,1,0:T(8,128)(2,1)} %bitcast.7, bf16[3,4,128,128]{3,2,1,0:T(8,128)(2,1)} %refs_2_.1, bf16[16,3,128,128]{3,2,1,0:T(8,128)(2,1)} %refs_3_.1, s32[3,16]{1,0:T(4,128)} %bitcast.8, ...), custom_call_target="tpu_custom_call" | custom-call | tf_op jit(solution)/shard_map/mesh_step/pallas_call | solution.py:833
  77.5 17.0 %write_results.1 = (bf16[16,128,128]{2,1,0:T(8,128)(2,1)}, f32[3,512,128]{2,1,0:T(8,128)}) custom-call(bf16[16,128,128]{2,1,0:T(8,128)(2,1)} %get-tuple-element.6.node_in, bf16[3,512,128]{2,1,0:T(8,128)(2,1)} %get-tuple-element.7.weight_in), custom_call_target="tpu_custom_call" | custom-call | tf_op jit(solution)/shard_map/write_results/pallas_call | solution.py:690

commit v4 on v3

--- a/solution.py
+++ b/solution.py
@@ -246,10 +246,6 @@
         + [at_y(i) for i in y_order]
         + [at_z(i) for i in z_order]
     )
-    barrier = pltpu.get_barrier_semaphore()
-    for partner in partners:
-        pl.semaphore_signal(barrier, inc=1, device_id=partner, device_id_type=MESH)
-
     started = []
 
     def send(src, dst, device):
@@ -276,6 +272,9 @@
 
     got_nodes = load(nodes, S.at[pl.ds(0, FB)])
     got_export = load(fine_export, fexport)
+    barrier = pltpu.get_barrier_semaphore()
+    for partner in partners:
+        pl.semaphore_signal(barrier, inc=1, device_id=partner, device_id_type=MESH)
     got_tcols = load(top_cols, tcols)
     got_pcols = load(pool_cols, pcols)
     got_ucols = load(upper_cols, ucols)
@@ -559,6 +558,7 @@
 
     for copy in mid_back:
         copy.wait_recv()
+    top_sum = shown_y(slot_sum(top_sum, W_Z.at[2], nz), W_Y.at[2])
     back_rows = jnp.concatenate(
         [MBACK_R[0] * has_left.astype(BF16), MBACK_R[1] * has_right.astype(BF16)], axis=0
     )
@@ -569,8 +569,6 @@
         for k in range(2):
             PPIECE[k * MB + m] = dot_at(PT[m, k], low)
     chain(PPIECE, pprev, 2 * MB)
-
-    top_sum = shown_y(slot_sum(top_sum, W_Z.at[2], nz), W_Y.at[2])
 
     WACC[...] = jnp.zeros_like(WACC)
 
@@ -591,10 +589,11 @@
             WACC[i] = WACC[i] + term
         return carry
 
-    lax.fori_loop(0, FB // GROUP, fine_backward, 0)
+    lax.fori_loop(0, FB // GROUP // 2, fine_backward, 0)
+    mid_sum = shown_z(scatter_sum(mid_sum, W_S.at[1], W_R.at[1]), W_Z.at[1])
+    lax.fori_loop(FB // GROUP // 2, FB // GROUP, fine_backward, 0)
     W_S[0] = flat(WACC[...]).astype(BF16)
     fine_sum = scattered(W_S.at[0], W_R.at[0])
-    mid_sum = shown_y(scatter_sum(mid_sum, W_S.at[1], W_R.at[1]), W_Y.at[1])
 
     def fine_rows(g, carry):
         here = pl.ds(g * GROUP, GROUP)
@@ -624,9 +623,9 @@
     value = scatter_sum(fine_sum, W_S.at[0], W_R.at[0])
     first = shown_y(value[0:half], W_Y.at[0, :, 0:half])
     second = shown_z(value[half:rows], W_Z.at[0, :, half:rows])
-    mid_sum = shown_z(slot_sum(mid_sum, W_Y.at[1], ny), W_Z.at[1])
     W_O[2, chunk(0, 0)] = slot_sum(top_sum, W_Y.at[2], ny)
     top_sum = gathered(W_O.at[2])
+    mid_sum = shown_y(slot_sum(mid_sum, W_Z.at[1], nz), W_Y.at[1])
 
     for copy in back:
         copy.wait_recv()
@@ -641,13 +640,12 @@
         ).astype(BF16)
         return carry
 
-    lax.fori_loop(0, FB // 2, finish, 0)
+    lax.fori_loop(0, FB, finish, 0)
     first = shown_z(slot_sum(first, W_Y.at[0, :, 0:half], ny), W_Z.at[0, :, 0:half])
     second = shown_y(slot_sum(second, W_Z.at[0, :, half:rows], nz), W_Y.at[0, :, half:rows])
-    W_O[1, chunk(0, 0)] = slot_sum(mid_sum, W_Z.at[1], nz)
+    put_nodes = load(ONODE, node_grad)
+    W_O[1, chunk(0, 0)] = slot_sum(mid_sum, W_Y.at[1], ny)
     mid_sum = gathered(W_O.at[1])
-    lax.fori_loop(FB // 2, FB, finish, 0)
-    put_nodes = load(ONODE, node_grad)
     W_O[0, chunk(0, 0)] = jnp.concatenate(
         [
             slot_sum(first, W_Z.at[0, :, 0:half], nz),
@@ -669,20 +667,23 @@
     put_fine.wait()
 
 
-def write_kernel(node_in, weight_in, node_out, weight_out, low, full, sem):
-    nodes = pltpu.make_async_copy(node_in, node_out, sem.at[0])
-    nodes.start()
-    fetch = [pltpu.make_async_copy(weight_in.at[l], low.at[l], sem.at[1 + l]) for l in range(3)]
-    put = [pltpu.make_async_copy(full.at[l], weight_out.at[l], sem.at[4 + l]) for l in range(3)]
+def write_kernel(node_in, weight_in, node_out, weight_out, nodes, low, full, sem):
+    fetch = [pltpu.make_async_copy(weight_in.at[l], low.at[l], sem.at[l]) for l in range(3)]
+    put = [pltpu.make_async_copy(full.at[l], weight_out.at[l], sem.at[3 + l]) for l in range(3)]
+    node_fetch = pltpu.make_async_copy(node_in, nodes, sem.at[6])
+    node_put = pltpu.make_async_copy(nodes, node_out, sem.at[7])
     for copy in fetch:
         copy.start()
+    node_fetch.start()
     for l in range(3):
         fetch[l].wait()
         full[l] = low[l].astype(F32)
         put[l].start()
+    node_fetch.wait()
+    node_put.start()
     for copy in put:
         copy.wait()
-    nodes.wait()
+    node_put.wait()
 
 
 def written(node_grad, weight_grad):
@@ -696,9 +697,10 @@
         in_specs=[anywhere] * 2,
         out_specs=(anywhere, anywhere),
         scratch_shapes=[
+            pltpu.VMEM(node_grad.shape, BF16),
             pltpu.VMEM(weight_grad.shape, BF16),
             pltpu.VMEM(weight_grad.shape, F32),
-            pltpu.SemaphoreType.DMA((7,)),
+            pltpu.SemaphoreType.DMA((8,)),
         ],
         compiler_params=pltpu.CompilerParams(vmem_limit_bytes=64 * 1024 * 1024),
         name="write_results",

time: 94.7 us -> 81.3 us (0.86)
  Pallas kernels: 93.9 us -> 80.5 us
    pallas_call x1, Pallas kernels: 17 us -> 2.1 us  [written(): pl.pallas_call(write_kernel, out_shape=(jax.ShapeDtypeStruct(node_grad.sh...]
    pallas_call x1, Pallas kernels: 76.8 us -> 78.4 us  [on_device(): pl.pallas_call(body, out_shape=(jax.ShapeDtypeStruct((FB, T, T), BF16), j...]
where the time goes in v4:
time: 81.3 us; the launch traced here: 81.1 us
  Pallas kernels  80.5 us (99%)
    pallas_call x1, Pallas kernels, on_device(): pl.pallas_call(body, out_shape=(jax.ShapeDtypeStruct((FB, T, T), BF16), j...  78.4 us
    pallas_call x1, Pallas kernels, written(): pl.pallas_call(write_kernel, out_shape=(jax.ShapeDtypeStruct(node_grad.sh...  2.1 us

profile of v4, /device:TPU:1, one launch (start us, length us, event | category | flops | bytes accessed | tf_op | source)
XLA Modules:
  0.0 81.1 jit_solution(11208207278367794815)
XLA Ops:
  0.6 78.4 %mesh_step.1 = (bf16[16,128,128]{2,1,0:T(8,128)(2,1)}, bf16[3,512,128]{2,1,0:T(8,128)(2,1)}) custom-call(bf16[16,128,128]{2,1,0:T(8,128)(2,1)} %bitcast.6, bf16[16,128,128]{2,1,0:T(8,128)(2,1)} %bitcast.7, bf16[3,4,128,128]{3,2,1,0:T(8,128)(2,1)} %refs_2_.1, bf16[16,3,128,128]{3,2,1,0:T(8,128)(2,1)} %refs_3_.1, s32[3,16]{1,0:T(4,128)} %bitcast.8, ...), custom_call_target="tpu_custom_call" | custom-call | tf_op jit(solution)/shard_map/mesh_step/pallas_call | solution.py:835
  79.0 2.1 %write_results.1 = (bf16[16,128,128]{2,1,0:T(8,128)(2,1)}, f32[3,512,128]{2,1,0:T(8,128)}) custom-call(bf16[16,128,128]{2,1,0:T(8,128)(2,1)} %get-tuple-element.6.node_in, bf16[3,512,128]{2,1,0:T(8,128)(2,1)} %get-tuple-element.7.weight_in), custom_call_target="tpu_custom_call" | custom-call | tf_op jit(solution)/shard_map/write_results/pallas_call | solution.py:691

commit v5 on v4

--- a/solution.py
+++ b/solution.py
@@ -558,7 +558,6 @@
 
     for copy in mid_back:
         copy.wait_recv()
-    top_sum = shown_y(slot_sum(top_sum, W_Z.at[2], nz), W_Y.at[2])
     back_rows = jnp.concatenate(
         [MBACK_R[0] * has_left.astype(BF16), MBACK_R[1] * has_right.astype(BF16)], axis=0
     )
@@ -589,11 +588,11 @@
             WACC[i] = WACC[i] + term
         return carry
 
-    lax.fori_loop(0, FB // GROUP // 2, fine_backward, 0)
-    mid_sum = shown_z(scatter_sum(mid_sum, W_S.at[1], W_R.at[1]), W_Z.at[1])
-    lax.fori_loop(FB // GROUP // 2, FB // GROUP, fine_backward, 0)
+    lax.fori_loop(0, FB // GROUP, fine_backward, 0)
     W_S[0] = flat(WACC[...]).astype(BF16)
     fine_sum = scattered(W_S.at[0], W_R.at[0])
+    top_sum = shown_y(slot_sum(top_sum, W_Z.at[2], nz), W_Y.at[2])
+    mid_sum = shown_z(scatter_sum(mid_sum, W_S.at[1], W_R.at[1]), W_Z.at[1])
 
     def fine_rows(g, carry):
         here = pl.ds(g * GROUP, GROUP)
@@ -627,6 +626,9 @@
     top_sum = gathered(W_O.at[2])
     mid_sum = shown_y(slot_sum(mid_sum, W_Z.at[1], nz), W_Y.at[1])
 
+    first = shown_z(slot_sum(first, W_Y.at[0, :, 0:half], ny), W_Z.at[0, :, 0:half])
+    second = shown_y(slot_sum(second, W_Z.at[0, :, half:rows], nz), W_Y.at[0, :, half:rows])
+
     for copy in back:
         copy.wait_recv()
     back_rows = jnp.concatenate(
@@ -641,8 +643,6 @@
         return carry
 
     lax.fori_loop(0, FB, finish, 0)
-    first = shown_z(slot_sum(first, W_Y.at[0, :, 0:half], ny), W_Z.at[0, :, 0:half])
-    second = shown_y(slot_sum(second, W_Z.at[0, :, half:rows], nz), W_Y.at[0, :, half:rows])
     put_nodes = load(ONODE, node_grad)
     W_O[1, chunk(0, 0)] = slot_sum(mid_sum, W_Y.at[1], ny)
     mid_sum = gathered(W_O.at[1])

time: 81.3 us -> 80.2 us (0.986)
  Pallas kernels: 80.5 us -> 79.4 us
    pallas_call x1, Pallas kernels: 78.4 us -> 77.3 us  [on_device(): pl.pallas_call(body, out_shape=(jax.ShapeDtypeStruct((FB, T, T), BF16), j...]
where the time goes in v5:
time: 80.2 us; the launch traced here: 80 us
  Pallas kernels  79.4 us (99%)
    pallas_call x1, Pallas kernels, on_device(): pl.pallas_call(body, out_shape=(jax.ShapeDtypeStruct((FB, T, T), BF16), j...  77.3 us
    pallas_call x1, Pallas kernels, written(): pl.pallas_call(write_kernel, out_shape=(jax.ShapeDtypeStruct(node_grad.sh...  2.1 us

profile of v5, /device:TPU:1, one launch (start us, length us, event | category | flops | bytes accessed | tf_op | source)
XLA Modules:
  0.0 80.0 jit_solution(15530476932376513172)
XLA Ops:
  0.6 77.3 %mesh_step.1 = (bf16[16,128,128]{2,1,0:T(8,128)(2,1)}, bf16[3,512,128]{2,1,0:T(8,128)(2,1)}) custom-call(bf16[16,128,128]{2,1,0:T(8,128)(2,1)} %bitcast.6, bf16[16,128,128]{2,1,0:T(8,128)(2,1)} %bitcast.7, bf16[3,4,128,128]{3,2,1,0:T(8,128)(2,1)} %refs_2_.1, bf16[16,3,128,128]{3,2,1,0:T(8,128)(2,1)} %refs_3_.1, s32[3,16]{1,0:T(4,128)} %bitcast.8, ...), custom_call_target="tpu_custom_call" | custom-call | tf_op jit(solution)/shard_map/mesh_step/pallas_call | solution.py:835
  77.9 2.1 %write_results.1 = (bf16[16,128,128]{2,1,0:T(8,128)(2,1)}, f32[3,512,128]{2,1,0:T(8,128)}) custom-call(bf16[16,128,128]{2,1,0:T(8,128)(2,1)} %get-tuple-element.6.node_in, bf16[3,512,128]{2,1,0:T(8,128)(2,1)} %get-tuple-element.7.weight_in), custom_call_target="tpu_custom_call" | custom-call | tf_op jit(solution)/shard_map/write_results/pallas_call | solution.py:691

commit v6 on v5

--- a/solution.py
+++ b/solution.py
@@ -8,6 +8,7 @@
 NY = 8
 NC = 2
 T = 128
+HALF = T // 2
 FB, MB, TB = 16, 4, 1
 GROUP = 4
 F32, BF16 = jnp.float32, jnp.bfloat16
@@ -189,16 +190,23 @@
     MBACK_R,
     COL_S,
     COL_R,
+    COLY_R,
     YG,
+    XG,
     PARTNER,
     SEL_S,
     SEL_R,
+    SELY_S,
+    SELY_R,
     P1_S,
     P1_R,
     P2_S,
     P2_R,
+    P2Y_R,
     PY_S,
     PY_R,
+    PX_S,
+    PX_R,
     WACC,
     W_S,
     W_R,
@@ -342,7 +350,8 @@
     halo = [send(HALO_S.at[1], HALO_R.at[0], right), send(HALO_S.at[0], HALO_R.at[1], left)]
     got_tcols.wait()
     COL_S[...] = jnp.full((8, T), tcols[0, 2], jnp.int32)
-    cols_sent = [send(COL_S, COL_R.at[i - 1], at_x(i)) for i in range(1, nx)]
+    cols_sent = [send(COL_S, COL_R.at[i - 1], at_x(i)) for i in x_order]
+    cols_sent += [send(COL_S, COLY_R.at[i - 1], at_y(i)) for i in y_order]
 
     for copy in (got_cot, got_pool, got_pcols, got_upper, got_ucols):
         copy.wait()
@@ -435,9 +444,11 @@
     MOUT[...] = tiled((mu.astype(F32) + dot(act2, mm[3])).astype(BF16))
     top_in = (dot(UT[0, 0], MOUT[ucols[0, 0]]) + dot(UT[0, 1], MOUT[ucols[0, 1]])).astype(BF16)
 
-    YG[0] = top_in
+    YG[0] = top_in[0:HALF]
+    XG[0] = top_in[HALF:T]
     along_y = [send(YG.at[0], YG.at[i], at_y(i)) for i in y_order]
-    half = send(YG.at[0], PARTNER, at_x(nx // 2))
+    along_x = [send(XG.at[0], XG.at[i], at_x(i)) for i in x_order]
+    partner = send(YG.at[0], PARTNER, at_x(nx // 2))
     MMSG[...] = tiled(mv)
     MACT1[...] = tiled(act1)
     MACT2[...] = tiled(act2)
@@ -457,29 +468,42 @@
     for copy in cols_sent:
         copy.wait_recv()
     cols = [COL_S[0:1]] + [COL_R[i, 0:1] for i in range(nx - 1)]
+    cols_y = [COL_S[0:1]] + [COLY_R[i, 0:1] for i in range(ny - 1)]
+
+    def chosen(column, blocks, sources):
+        total = jnp.zeros((HALF, T), BF16)
+        for k, source in enumerate(sources):
+            total = total + jnp.where(column == source, 1.0, 0.0).astype(BF16) * blocks[k]
+        return total
+
+    by_x = [lax.rem(x + nx - k, nx) * ny + y for k in range(nx)]
+    by_y = [x * ny + lax.rem(y + ny - k, ny) for k in range(ny)]
+    for copy in along_x:
+        copy.wait_recv()
+    chosen_y = []
+    for i in y_order:
+        SELY_S[i - 1] = chosen(cols_y[ny - i], XG, by_x)
+        chosen_y.append(send(SELY_S.at[i - 1], SELY_R.at[i - 1], at_y(i)))
+    lower = chosen(cols[0], XG, by_x)
     for copy in along_y:
         copy.wait_recv()
-
-    def chosen(column):
-        total = jnp.zeros((T, T), BF16)
-        for k in range(ny):
-            source = x * ny + lax.rem(y + ny - k, ny)
-            total = total + jnp.where(column == source, 1.0, 0.0).astype(BF16) * YG[k]
-        return total
-
-    along_x = []
+    chosen_x = []
     for i in x_order:
-        SEL_S[i - 1] = chosen(cols[nx - i])
-        along_x.append(send(SEL_S.at[i - 1], SEL_R.at[i - 1], at_x(i)))
-    third = chosen(cols[0])
-    half.wait_recv()
-    top_part = top_part + dot(TT[0, 1], PARTNER[...])
+        SEL_S[i - 1] = chosen(cols[nx - i], YG, by_y)
+        chosen_x.append(send(SEL_S.at[i - 1], SEL_R.at[i - 1], at_x(i)))
+    upper = chosen(cols[0], YG, by_y)
+    partner.wait_recv()
+    across = jnp.concatenate([PARTNER[...], XG[nx // 2]], axis=0)
+    top_part = top_part + dot(TT[0, 1], across)
     link(lambda s: pcols[lax.div(s, MB), lax.rem(s, MB)], 2 * MB, FB, pprev, plast)
     link(lambda s: mcols[lax.rem(s, MB), 1 + lax.div(s, MB)], 2 * MB, MB + 2, mprev, mlast)
-    for copy in along_x:
-        copy.wait_recv()
+    for copy in chosen_y + chosen_x:
+        copy.wait_recv()
+    for i in range(ny - 1):
+        lower = lower + SELY_R[i]
     for i in range(nx - 1):
-        third = third + SEL_R[i]
+        upper = upper + SEL_R[i]
+    third = jnp.concatenate([upper, lower], axis=0)
     top_msg = (top_part + dot(TT[0, 2], third)).astype(BF16)
     pre1, act1, pre2, act2 = forward(top_in, top_msg, top_own, tm)
 
@@ -498,7 +522,8 @@
 
     gb, gs, gf, gm = backward(grad_top, slope(pre1), slope(pre2), tm)
     P2_S[...] = dot_at(TT[0, 2], gm).astype(BF16)
-    back_x = [send(P2_S, P2_R.at[i - 1], at_x(i)) for i in x_order]
+    back_x = [send(P2_S.at[pl.ds(0, HALF)], P2_R.at[i - 1], at_x(i)) for i in x_order]
+    back_y = [send(P2_S.at[pl.ds(HALF, HALF)], P2Y_R.at[i - 1], at_y(i)) for i in y_order]
     P1_S[...] = dot_at(TT[0, 1], gm).astype(BF16)
     back_half = send(P1_S, P1_R, at_x(nx // 2))
     grad_top_in = grad_top + dot_bt(gf, tm[0]) + dot_at(TT[0, 0], gm)
@@ -506,27 +531,40 @@
         W_S[2, pl.ds(i * T, T)] = term.astype(BF16)
     for copy in back_x:
         copy.wait_recv()
-    arrived = [P2_S[...].astype(F32)] + [P2_R[i].astype(F32) for i in range(nx - 1)]
-
-    def summed(target):
-        total = jnp.zeros((T, T), F32)
-        for column, piece in zip(cols, arrived):
+    upper_parts = [P2_S[0:HALF].astype(F32)] + [P2_R[i].astype(F32) for i in range(nx - 1)]
+
+    def summed(target, columns, pieces):
+        total = jnp.zeros((HALF, T), F32)
+        for column, piece in zip(columns, pieces):
             total = total + jnp.where(column == target, 1.0, 0.0) * piece
         return total
 
-    back_y = []
+    summed_y = []
     for i in y_order:
-        PY_S[i - 1] = summed(x * ny + lax.rem(y + i, ny)).astype(BF16)
-        back_y.append(send(PY_S.at[i - 1], PY_R.at[i - 1], at_y(i)))
+        target = x * ny + lax.rem(y + i, ny)
+        PY_S[i - 1] = summed(target, cols, upper_parts).astype(BF16)
+        summed_y.append(send(PY_S.at[i - 1], PY_R.at[i - 1], at_y(i)))
+    upper = summed(dom, cols, upper_parts)
+    for copy in back_y:
+        copy.wait_recv()
+    lower_parts = [P2_S[HALF:T].astype(F32)] + [P2Y_R[i].astype(F32) for i in range(ny - 1)]
+    summed_x = []
+    for i in x_order:
+        target = lax.rem(x + i, nx) * ny + y
+        PX_S[i - 1] = summed(target, cols_y, lower_parts).astype(BF16)
+        summed_x.append(send(PX_S.at[i - 1], PX_R.at[i - 1], at_x(i)))
+    lower = summed(dom, cols_y, lower_parts)
     top_sum = scattered(W_S.at[2], W_R.at[2])
-    grad_top_in = grad_top_in + summed(dom)
     link(lambda s: fcols[1 + lax.div(s, FB), lax.rem(s, FB)], 2 * FB, FB + 2, fprev, flast)
     back_half.wait_recv()
     grad_top_in = grad_top_in + P1_R[...].astype(F32)
-    for copy in back_y:
+    for copy in summed_y + summed_x:
         copy.wait_recv()
     for i in range(ny - 1):
-        grad_top_in = grad_top_in + PY_R[i].astype(F32)
+        upper = upper + PY_R[i].astype(F32)
+    for i in range(nx - 1):
+        lower = lower + PX_R[i].astype(F32)
+    grad_top_in = grad_top_in + jnp.concatenate([upper, lower], axis=0)
 
     top_sum = shown_z(scatter_sum(top_sum, W_S.at[2], W_R.at[2]), W_Z.at[2])
 
@@ -741,8 +779,7 @@
     rows = 4 * T // (NC * nx)
     copies = (
         4 * 2
-        + (nx - 1) * 3
-        + (ny - 1) * 2
+        + (nx - 1 + ny - 1) * 5
         + 2
         + 3 * 2 * (NC * nx - 1)
         + 4 * (ny - 1 + nz - 1)
@@ -806,16 +843,23 @@
         low(2, T, T),
         pltpu.VMEM((8, T), jnp.int32),
         pltpu.VMEM((nx - 1, 8, T), jnp.int32),
-        low(ny, T, T),
-        low(T, T),
-        low(nx - 1, T, T),
-        low(nx - 1, T, T),
+        pltpu.VMEM((ny - 1, 8, T), jnp.int32),
+        low(ny, HALF, T),
+        low(nx, HALF, T),
+        low(HALF, T),
+        low(nx - 1, HALF, T),
+        low(nx - 1, HALF, T),
+        low(ny - 1, HALF, T),
+        low(ny - 1, HALF, T),
         low(T, T),
         low(T, T),
         low(T, T),
-        low(nx - 1, T, T),
-        low(ny - 1, T, T),
-        low(ny - 1, T, T),
+        low(nx - 1, HALF, T),
+        low(ny - 1, HALF, T),
+        low(ny - 1, HALF, T),
+        low(ny - 1, HALF, T),
+        low(nx - 1, HALF, T),
+        low(nx - 1, HALF, T),
         full(4, T, T),
         low(3, 4 * T, T),
         low(3, NC * nx - 1, rows, T),

time: 80.2 us -> 79.4 us (0.990)
  no operation moved by 1% of the time
where the time goes in v6:
time: 79.4 us; the launch traced here: 79.3 us
  Pallas kernels  78.6 us (99%)
    pallas_call x1, Pallas kernels, on_device(): pl.pallas_call(body, out_shape=(jax.ShapeDtypeStruct((FB, T, T), BF16), j...  76.5 us
    pallas_call x1, Pallas kernels, written(): pl.pallas_call(write_kernel, out_shape=(jax.ShapeDtypeStruct(node_grad.sh...  2.1 us

profile of v6, /device:TPU:1, one launch (start us, length us, event | category | flops | bytes accessed | tf_op | source)
XLA Modules:
  0.0 79.3 jit_solution(8153001196741595183)
XLA Ops:
  0.6 76.5 %mesh_step.1 = (bf16[16,128,128]{2,1,0:T(8,128)(2,1)}, bf16[3,512,128]{2,1,0:T(8,128)(2,1)}) custom-call(bf16[16,128,128]{2,1,0:T(8,128)(2,1)} %bitcast.6, bf16[16,128,128]{2,1,0:T(8,128)(2,1)} %bitcast.7, bf16[3,4,128,128]{3,2,1,0:T(8,128)(2,1)} %refs_2_.1, bf16[16,3,128,128]{3,2,1,0:T(8,128)(2,1)} %refs_3_.1, s32[3,16]{1,0:T(4,128)} %bitcast.8, ...), custom_call_target="tpu_custom_call" | custom-call | tf_op jit(solution)/shard_map/mesh_step/pallas_call | solution.py:879
  77.2 2.1 %write_results.1 = (bf16[16,128,128]{2,1,0:T(8,128)(2,1)}, f32[3,512,128]{2,1,0:T(8,128)}) custom-call(bf16[16,128,128]{2,1,0:T(8,128)(2,1)} %get-tuple-element.6.node_in, bf16[3,512,128]{2,1,0:T(8,128)(2,1)} %get-tuple-element.7.weight_in), custom_call_target="tpu_custom_call" | custom-call | tf_op jit(solution)/shard_map/write_results/pallas_call | solution.py:729

commit v7 on v6

--- a/solution.py
+++ b/solution.py
@@ -10,7 +10,7 @@
 T = 128
 HALF = T // 2
 FB, MB, TB = 16, 4, 1
-GROUP = 4
+GROUP = 8
 F32, BF16 = jnp.float32, jnp.bfloat16
 MESH = pl.DeviceIdType.MESH
 
@@ -80,7 +80,7 @@
     return dot(onehot, rows)
 
 
-def link(column, number, targets, prev, last):
+def link(column, number, targets, prev, last, parts=(True, True)):
     def before(s, carry):
         mine = column(s)
         best = jnp.int32(-1)
@@ -96,8 +96,10 @@
         last[j] = best
         return carry
 
-    lax.fori_loop(0, number, before, 0)
-    lax.fori_loop(0, targets, final, 0)
+    if parts[0]:
+        lax.fori_loop(0, number, before, 0)
+    if parts[1]:
+        lax.fori_loop(0, targets, final, 0)
 
 
 def linked(pieces, at):
@@ -283,6 +285,55 @@
     barrier = pltpu.get_barrier_semaphore()
     for partner in partners:
         pl.semaphore_signal(barrier, inc=1, device_id=partner, device_id_type=MESH)
+
+    has_left = jnp.where(dom > 0, 1.0, 0.0).astype(F32)
+    has_right = jnp.where(dom < ndom - 1, 1.0, 0.0).astype(F32)
+
+    def level(l):
+        return [M[l, i] for i in range(4)]
+
+    rows = 4 * T // (NC * nx)
+
+    def chunk(c, i):
+        number = lax.rem(core + c, NC) * nx + lax.rem(x + i, nx)
+        return pl.ds(pl.multiple_of(number * rows, rows), rows)
+
+    def scattered(store, slots):
+        return [
+            send(store.at[chunk(c, i)], slots.at[n], at_cx(c, i))
+            for n, (c, i) in enumerate(cx_order)
+        ]
+
+    def scatter_sum(copies, store, slots):
+        for copy in copies:
+            copy.wait_recv()
+        total = store[chunk(0, 0)].astype(F32)
+        for n in range(len(cx_order)):
+            total = total + slots[n].astype(F32)
+        return total.astype(BF16)
+
+    def shown_y(value, slots):
+        slots[y] = value
+        return [send(slots.at[y], slots.at[y], at_y(i)) for i in y_order]
+
+    def shown_z(value, slots):
+        slots[z] = value
+        return [send(slots.at[z], slots.at[z], at_z(i)) for i in z_order]
+
+    def slot_sum(copies, slots, number):
+        for copy in copies:
+            copy.wait_recv()
+        total = slots[0].astype(F32)
+        for i in range(1, number):
+            total = total + slots[i].astype(F32)
+        return total.astype(BF16)
+
+    def gathered(store):
+        mine = store.at[chunk(0, 0)]
+        return [send(mine, mine, at_cx(c, i)) for c, i in cx_order]
+
+    got_export.wait()
+    got_nodes.wait()
     got_tcols = load(top_cols, tcols)
     got_pcols = load(pool_cols, pcols)
     got_ucols = load(upper_cols, ucols)
@@ -296,55 +347,6 @@
     got_mcols = load(mid_cols, mcols)
     got_mexport = load(mid_export, mexport)
     got_top = load(top_tiles, TT)
-
-    has_left = jnp.where(dom > 0, 1.0, 0.0).astype(F32)
-    has_right = jnp.where(dom < ndom - 1, 1.0, 0.0).astype(F32)
-
-    def level(l):
-        return [M[l, i] for i in range(4)]
-
-    rows = 4 * T // (NC * nx)
-
-    def chunk(c, i):
-        number = lax.rem(core + c, NC) * nx + lax.rem(x + i, nx)
-        return pl.ds(pl.multiple_of(number * rows, rows), rows)
-
-    def scattered(store, slots):
-        return [
-            send(store.at[chunk(c, i)], slots.at[n], at_cx(c, i))
-            for n, (c, i) in enumerate(cx_order)
-        ]
-
-    def scatter_sum(copies, store, slots):
-        for copy in copies:
-            copy.wait_recv()
-        total = store[chunk(0, 0)].astype(F32)
-        for n in range(len(cx_order)):
-            total = total + slots[n].astype(F32)
-        return total.astype(BF16)
-
-    def shown_y(value, slots):
-        slots[y] = value
-        return [send(slots.at[y], slots.at[y], at_y(i)) for i in y_order]
-
-    def shown_z(value, slots):
-        slots[z] = value
-        return [send(slots.at[z], slots.at[z], at_z(i)) for i in z_order]
-
-    def slot_sum(copies, slots, number):
-        for copy in copies:
-            copy.wait_recv()
-        total = slots[0].astype(F32)
-        for i in range(1, number):
-            total = total + slots[i].astype(F32)
-        return total.astype(BF16)
-
-    def gathered(store):
-        mine = store.at[chunk(0, 0)]
-        return [send(mine, mine, at_cx(c, i)) for c, i in cx_order]
-
-    got_export.wait()
-    got_nodes.wait()
     HALO_S[...] = picked_rows(fexport[0], S.at[pl.ds(0, FB)])
     pl.semaphore_wait(barrier, len(partners))
     halo = [send(HALO_S.at[1], HALO_R.at[0], right), send(HALO_S.at[0], HALO_R.at[1], left)]
@@ -427,6 +429,12 @@
         MPART[r] = dot(MT[r, 0], MS[r])
     got_top.wait()
     link(lambda s: ucols[0, s], 2, MB, uprev, ulast)
+
+    def fine_links(*parts):
+        column = lambda s: fcols[1 + lax.div(s, FB), lax.rem(s, FB)]
+        link(column, 2 * FB, FB + 2, fprev, flast, parts)
+
+    fine_links(True, False)
     for copy in mid_halo:
         copy.wait_recv()
     MS[MB] = MHALO_R[0] * has_left.astype(BF16)
@@ -497,6 +505,7 @@
     top_part = top_part + dot(TT[0, 1], across)
     link(lambda s: pcols[lax.div(s, MB), lax.rem(s, MB)], 2 * MB, FB, pprev, plast)
     link(lambda s: mcols[lax.rem(s, MB), 1 + lax.div(s, MB)], 2 * MB, MB + 2, mprev, mlast)
+    fine_links(False, True)
     for copy in chosen_y + chosen_x:
         copy.wait_recv()
     for i in range(ny - 1):
@@ -555,7 +564,6 @@
         summed_x.append(send(PX_S.at[i - 1], PX_R.at[i - 1], at_x(i)))
     lower = summed(dom, cols_y, lower_parts)
     top_sum = scattered(W_S.at[2], W_R.at[2])
-    link(lambda s: fcols[1 + lax.div(s, FB), lax.rem(s, FB)], 2 * FB, FB + 2, fprev, flast)
     back_half.wait_recv()
     grad_top_in = grad_top_in + P1_R[...].astype(F32)
     for copy in summed_y + summed_x:
@@ -607,6 +615,7 @@
             PPIECE[k * MB + m] = dot_at(PT[m, k], low)
     chain(PPIECE, pprev, 2 * MB)
 
+    top_sum = shown_y(slot_sum(top_sum, W_Z.at[2], nz), W_Y.at[2])
     WACC[...] = jnp.zeros_like(WACC)
 
     def fine_backward(g, carry):
@@ -629,7 +638,6 @@
     lax.fori_loop(0, FB // GROUP, fine_backward, 0)
     W_S[0] = flat(WACC[...]).astype(BF16)
     fine_sum = scattered(W_S.at[0], W_R.at[0])
-    top_sum = shown_y(slot_sum(top_sum, W_Z.at[2], nz), W_Y.at[2])
     mid_sum = shown_z(scatter_sum(mid_sum, W_S.at[1], W_R.at[1]), W_Z.at[1])
 
     def fine_rows(g, carry):
@@ -642,15 +650,15 @@
     lax.fori_loop(0, FB // GROUP, fine_rows, 0)
 
     def fine_pieces(g, carry):
-        for b in range(2):
-            r = g * 2 + b
+        for b in range(4):
+            r = g * 4 + b
             grad = GM[r]
             PIECE[r] = dot_at(FT[r, 1], grad)
             PIECE[FB + r] = dot_at(FT[r, 2], grad)
             GN[r] = GN[r] + dot_at(FT[r, 0], grad)
         return carry
 
-    lax.fori_loop(0, FB // 2, fine_pieces, 0)
+    lax.fori_loop(0, FB // 4, fine_pieces, 0)
     chain(PIECE, fprev, 2 * FB)
     BACK_S[0] = linked(PIECE, flast[FB]).astype(BF16)
     BACK_S[1] = linked(PIECE, flast[FB + 1]).astype(BF16)
@@ -674,13 +682,15 @@
     )
     fexp = fexport[0]
 
-    def finish(r, carry):
-        ONODE[r] = (
-            GN[r] + linked(PIECE, flast[r]) + placed_rows(fexp, r, back_rows)
-        ).astype(BF16)
+    def finish(g, carry):
+        for b in range(4):
+            r = g * 4 + b
+            ONODE[r] = (
+                GN[r] + linked(PIECE, flast[r]) + placed_rows(fexp, r, back_rows)
+            ).astype(BF16)
         return carry
 
-    lax.fori_loop(0, FB, finish, 0)
+    lax.fori_loop(0, FB // 4, finish, 0)
     put_nodes = load(ONODE, node_grad)
     W_O[1, chunk(0, 0)] = slot_sum(mid_sum, W_Y.at[1], ny)
     mid_sum = gathered(W_O.at[1])

time: 79.4 us -> 76.3 us (0.961)
  Pallas kernels: 78.6 us -> 75.5 us
    pallas_call x1, Pallas kernels: 76.5 us -> 73.4 us  [on_device(): pl.pallas_call(body, out_shape=(jax.ShapeDtypeStruct((FB, T, T), BF16), j...]
where the time goes in v7:
time: 76.3 us; the launch traced here: 76.1 us
  Pallas kernels  75.5 us (99%)
    pallas_call x1, Pallas kernels, on_device(): pl.pallas_call(body, out_shape=(jax.ShapeDtypeStruct((FB, T, T), BF16), j...  73.4 us
    pallas_call x1, Pallas kernels, written(): pl.pallas_call(write_kernel, out_shape=(jax.ShapeDtypeStruct(node_grad.sh...  2.1 us

profile of v7, /device:TPU:1, one launch (start us, length us, event | category | flops | bytes accessed | tf_op | source)
XLA Modules:
  0.0 76.1 jit_solution(12828539217084559858)
XLA Ops:
  0.6 73.4 %mesh_step.1 = (bf16[16,128,128]{2,1,0:T(8,128)(2,1)}, bf16[3,512,128]{2,1,0:T(8,128)(2,1)}) custom-call(bf16[16,128,128]{2,1,0:T(8,128)(2,1)} %bitcast.6, bf16[16,128,128]{2,1,0:T(8,128)(2,1)} %bitcast.7, bf16[3,4,128,128]{3,2,1,0:T(8,128)(2,1)} %refs_2_.1, bf16[16,3,128,128]{3,2,1,0:T(8,128)(2,1)} %refs_3_.1, s32[3,16]{1,0:T(4,128)} %bitcast.8, ...), custom_call_target="tpu_custom_call" | custom-call | tf_op jit(solution)/shard_map/mesh_step/pallas_call | solution.py:889
  74.0 2.1 %write_results.1 = (bf16[16,128,128]{2,1,0:T(8,128)(2,1)}, f32[3,512,128]{2,1,0:T(8,128)}) custom-call(bf16[16,128,128]{2,1,0:T(8,128)(2,1)} %get-tuple-element.6.node_in, bf16[3,512,128]{2,1,0:T(8,128)(2,1)} %get-tuple-element.7.weight_in), custom_call_target="tpu_custom_call" | custom-call | tf_op jit(solution)/shard_map/write_results/pallas_call | solution.py:739
